TPU v7x, 512 devices: a whole 4x8x8 slice. The times are simulated.
512 devices in a mesh: col: 64 (over z, y_hi, core), row: 8 (over y_lo, x).
Axes of the slice: x: 4, y: 8 (y_hi: 4, y_lo: 2; y = y_hi * 2 + y_lo), z: 8, core: 2. Of those that a mesh axis runs over, the one named last changes fastest.
Arguments:
- decoded: bfloat16 [3, 256, 8192], P(None, 'row', 'col'), may hold values from -6 to 6
- loop_in: bfloat16 [9, 32, 3], replicated, may hold values from -1.25 to 1.25
- loop_out: bfloat16 [9, 3, 32], replicated, may hold values from -0.375 to 0.375
- first_conv: bfloat16 [9, 64, 3], replicated, may hold values from -1.25 to 1.25
- dense_first: bfloat16 [9, 32, 64], replicated, may hold values from -0.25 to 0.25
- dense_second: bfloat16 [9, 32, 96], replicated, may hold values from -0.21875 to 0.21875
- dense_third: bfloat16 [9, 32, 128], replicated, may hold values from -0.1875 to 0.1875
- dense_fourth: bfloat16 [9, 32, 160], replicated, may hold values from -0.15625 to 0.15625
- dense_fifth: bfloat16 [9, 64, 192], replicated, may hold values from -0.15625 to 0.15625
- head_conv: bfloat16 [9, 12, 64], replicated, may hold values from -0.25 to 0.25
Outputs:
- upscaled: float32 [8, 64, 3, 16384], P('row', 'col')
All inputs are finite; a program needn't handle non-finite values.
Results may differ from a plain program's by a relative error of at most 0.005.
Values may be sent and summed in bfloat16 or wider, within the bound.
No kernel may reach another device: no remote copies, remote signals or barrier semaphores. Data moves between devices by JAX's collectives and lax.ppermute only.
A program may use at most 128 MiB of HBM per device.

v0:
```python
import jax
import jax.numpy as jnp
from jax import lax
from jax.sharding import PartitionSpec as P


def shortened(array):
    return jax.tree.map(lambda a: a.astype(jnp.bfloat16) if a.dtype == jnp.float32 else a, array)


def padded_2(block, sides, width):
    for axis, dim in sides:
        count = lax.axis_size(axis)
        forward = [(i, i + 1) for i in range(count - 1)]
        backward = [(target, source) for source, target in forward]
        low = lax.ppermute(
            lax.slice_in_dim(block, block.shape[dim] - width, None, axis=dim), axis, forward
        )
        high = lax.ppermute(lax.slice_in_dim(block, 0, width, axis=dim), axis, backward)
        block = jnp.concatenate([low, block, high], axis=dim)
    return block


def leaky_relu(values):
    return jnp.where(values >= 0, values, 0.2 * values)


def conv_valid(padded, weight):
    kernel = weight.reshape(3, 3, weight.shape[1], weight.shape[2]).transpose(2, 3, 0, 1)
    result = lax.conv_general_dilated(
        padded[None],
        kernel,
        (1, 1),
        "VALID",
        dimension_numbers=("NCHW", "OIHW", "NCHW"),
        preferred_element_type=jnp.float32,
    )
    return result[0]


def conv_pieces(pieces, weight):
    summed = None
    offset = 0
    for member in pieces:
        channels = member.shape[0]
        term = conv_valid(member, weight[:, :, offset : offset + channels])
        summed = term if summed is None else summed + term
        offset = offset + channels
    return summed


def network(decoded, weights, prepare, clip_frame):
    loop_in, loop_out, first_conv, dense_list, head_conv = weights
    hidden = clip_frame(leaky_relu(conv_pieces([prepare(decoded)], loop_in))).astype(jnp.bfloat16)
    filtered = clip_frame(
        decoded.astype(jnp.float32) + conv_pieces([prepare(hidden)], loop_out)
    ).astype(jnp.bfloat16)
    features = clip_frame(conv_pieces([prepare(filtered)], first_conv)).astype(jnp.bfloat16)
    pieces = [prepare(features)]
    for layer in range(4):
        dense_out = clip_frame(leaky_relu(conv_pieces(pieces, dense_list[layer]))).astype(
            jnp.bfloat16
        )
        pieces.append(prepare(dense_out))
    block_out = clip_frame(
        features.astype(jnp.float32) + 0.2 * conv_pieces(pieces, dense_list[4])
    ).astype(jnp.bfloat16)
    return conv_pieces([prepare(block_out)], head_conv)


def edge_rim(field):
    return padded_2(shortened(field), (("col", 2), ("row", 1)), 1).astype(field.dtype)


def keep_all(values):
    return values


def on_device(
    decoded,
    loop_in,
    loop_out,
    first_conv,
    dense_first,
    dense_second,
    dense_third,
    dense_fourth,
    dense_fifth,
    head_conv,
):
    weights = (
        loop_in,
        loop_out,
        first_conv,
        (dense_first, dense_second, dense_third, dense_fourth, dense_fifth),
        head_conv,
    )
    planes = decoded.shape[0]
    height = decoded.shape[1]
    breadth = decoded.shape[2]
    head_out = network(decoded, weights, edge_rim, keep_all)
    col_count = lax.axis_size("col")
    band_rows = 2 * height // col_count
    doubled = head_out.reshape(planes, 2, 2, height, breadth).transpose(0, 3, 1, 4, 2)
    doubled = doubled.reshape(planes, 2 * height, 2 * breadth)
    outgoing = doubled.reshape(planes, col_count, band_rows, 2 * breadth).transpose(1, 2, 0, 3)
    return lax.all_to_all(outgoing, "col", split_axis=0, concat_axis=3, tiled=True)


def solution(mesh):
    in_specs = (P(None, "row", "col"), P(), P(), P(), P(), P(), P(), P(), P(), P())
    out_specs = P("row", "col", None, None)
    return jax.shard_map(
        on_device, mesh=mesh, in_specs=in_specs, out_specs=out_specs, check_vma=False
    )
```

profile of v0, /device:TPU:7, one launch (start us, length us, event | category | flops | bytes accessed | tf_op | source)
XLA Modules:
  0.0 317.0 jit_solution(7479465286400003795)
XLA Ops:
  0.9 4.8 %collective-permute-start = (bf16[3,32,1]{2,1,0:T(8,128)(2,1)S(1)}, bf16[3,32,1]{2,1,0:T(8,128)(2,1)S(1)}, u32[]{:S(2)}, u32[]{:S(2)}) collective-permute-start(bf16[3,32,1]{2,1,0:T(8,128)(2,1)S(1)} %get-tuple-element.48), channel_id=1, source_target_pairs={{0,8},{8,16},{16,24},{24,32},{32,40},{40,48},{48,56},{56,64},{64,7... | collective-permute-start | bytes 584 | tf_op jit(solution)/shard_map/ppermute | solution.py:16
  7.6 4.1 %collective-permute-done.1 = bf16[3,32,1]{2,1,0:T(8,128)(2,1)S(1)} collective-permute-done((bf16[3,32,1]{2,1,0:T(8,128)(2,1)S(1)}, bf16[3,32,1]{2,1,0:T(8,128)(2,1)S(1)}, u32[]{:S(2)}, u32[]{:S(2)}) %collective-permute-start.1) | collective-permute-done | bytes 224 | tf_op jit(solution)/shard_map/ppermute | solution.py:19
  12.5 3.1 collective-permute-start.2
  17.8 4.3 %collective-permute-done.3 = bf16[3,1,130]{2,1,0:T(2,128)(2,1)S(1)} collective-permute-done((bf16[3,1,130]{2,1,0:T(2,128)(2,1)S(1)}, bf16[3,1,130]{2,1,0:T(2,128)(2,1)S(1)}, u32[]{:S(2)}, u32[]{:S(2)}) %collective-permute-start.3) | collective-permute-done | bytes 812 | tf_op jit(solution)/shard_map/ppermute | solution.py:19
  27.5 3.4 %collective-permute-start.4 = (bf16[32,32,1]{0,1,2:T(8,128)(2,1)S(1)}, bf16[32,32,1]{0,1,2:T(8,128)(2,1)S(1)}, u32[]{:S(2)}, u32[]{:S(2)}) collective-permute-start(bf16[32,32,1]{0,1,2:T(8,128)(2,1)S(1)} %get-tuple-element.31), channel_id=1, source_target_pairs={{0,8},{8,16},{16,24},{24,32},{32,40},{40,48},{48,56},{56,64},{64,7... | collective-permute-start | bytes 6152 | tf_op jit(solution)/shard_map/ppermute | solution.py:16
  32.8 4.2 %collective-permute-done.5 = bf16[32,32,1]{0,1,2:T(8,128)(2,1)S(1)} collective-permute-done((bf16[32,32,1]{0,1,2:T(8,128)(2,1)S(1)}, bf16[32,32,1]{0,1,2:T(8,128)(2,1)S(1)}, u32[]{:S(2)}, u32[]{:S(2)}) %collective-permute-start.5) | collective-permute-done | bytes 2080 | tf_op jit(solution)/shard_map/ppermute | solution.py:19
  39.0 3.7 %collective-permute-start.7 = (bf16[32,1,130]{0,1,2:T(2,128)(2,1)S(1)}, bf16[32,1,130]{0,1,2:T(2,128)(2,1)S(1)}, u32[]{:S(2)}, u32[]{:S(2)}) collective-permute-start(bf16[32,1,130]{0,1,2:T(2,128)(2,1)S(1)} %get-tuple-element.18), channel_id=1, source_target_pairs={{1,0},{2,1},{3,2},{4,3},{5,4},{6,5},{7,6},{9,8},{10,9},{11,10},{12... | collective-permute-start | bytes 24968 | tf_op jit(solution)/shard_map/ppermute | solution.py:19
  42.7 3.5 %collective-permute-done.7 = bf16[32,1,130]{0,1,2:T(2,128)(2,1)S(1)} collective-permute-done((bf16[32,1,130]{0,1,2:T(2,128)(2,1)S(1)}, bf16[32,1,130]{0,1,2:T(2,128)(2,1)S(1)}, u32[]{:S(2)}, u32[]{:S(2)}) %collective-permute-start.7) | collective-permute-done | bytes 8352 | tf_op jit(solution)/shard_map/ppermute | solution.py:19
  47.9 24.5 %fusion.44 = f32[32,8,17,3]{1,3,2,0:T(4,128)S(1)} fusion(bf16[3,3,3,32]{3,2,1,0:T(4,128)(2,1)S(1)} %bitcast.229, bf16[32,34,1,7,2]{0,3,4,1,2:T(8,128)(2,1)S(1)} %slice.232, bf16[32,34,1,8,17]{0,3,4,1,2:T(8,128)(2,1)S(1)} %copy.246, pred[8,17]{0,1:T(8,128)(4,1)S(1)} %copy-done.10), kind=kOutput, calls=%fused_computation.70 | convolution fusion | flops 8525568 | bytes 380488 | tf_op jit(solution)/shard_map/conv_general_dilated | solution.py:30
  73.3 3.7 %collective-permute-start.8 = (bf16[3,32,1]{2,1,0:T(8,128)(2,1)S(1)}, bf16[3,32,1]{2,1,0:T(8,128)(2,1)S(1)}, u32[]{:S(2)}, u32[]{:S(2)}) collective-permute-start(bf16[3,32,1]{2,1,0:T(8,128)(2,1)S(1)} %get-tuple-element.46), channel_id=1, source_target_pairs={{0,8},{8,16},{16,24},{24,32},{32,40},{40,48},{48,56},{56,64},{64,7... | collective-permute-start | bytes 584 | tf_op jit(solution)/shard_map/ppermute | solution.py:16
  79.0 4.8 %collective-permute-done.9 = bf16[3,32,1]{2,1,0:T(8,128)(2,1)S(1)} collective-permute-done((bf16[3,32,1]{2,1,0:T(8,128)(2,1)S(1)}, bf16[3,32,1]{2,1,0:T(8,128)(2,1)S(1)}, u32[]{:S(2)}, u32[]{:S(2)}) %collective-permute-start.9) | collective-permute-done | bytes 224 | tf_op jit(solution)/shard_map/ppermute | solution.py:19
  85.8 3.9 %collective-permute-start.11 = (bf16[3,1,130]{2,1,0:T(2,128)(2,1)S(1)}, bf16[3,1,130]{2,1,0:T(2,128)(2,1)S(1)}, u32[]{:S(2)}, u32[]{:S(2)}) collective-permute-start(bf16[3,1,130]{2,1,0:T(2,128)(2,1)S(1)} %get-tuple-element.43), channel_id=1, source_target_pairs={{1,0},{2,1},{3,2},{4,3},{5,4},{6,5},{7,6},{9,8},{10,9},{11,10},{12... | collective-permute-start | bytes 2348 | tf_op jit(solution)/shard_map/ppermute | solution.py:19
  95.9 3.4 %collective-permute-start.12 = (bf16[64,32,1]{0,1,2:T(8,128)(2,1)S(1)}, bf16[64,32,1]{0,1,2:T(8,128)(2,1)S(1)}, u32[]{:S(2)}, u32[]{:S(2)}) collective-permute-start(bf16[64,32,1]{0,1,2:T(8,128)(2,1)S(1)} %get-tuple-element.29), channel_id=1, source_target_pairs={{0,8},{8,16},{16,24},{24,32},{32,40},{40,48},{48,56},{56,64},{64,7... | collective-permute-start | bytes 12296 | tf_op jit(solution)/shard_map/ppermute | solution.py:16
  101.4 4.7 %collective-permute-done.13 = bf16[64,32,1]{0,1,2:T(8,128)(2,1)S(1)} collective-permute-done((bf16[64,32,1]{0,1,2:T(8,128)(2,1)S(1)}, bf16[64,32,1]{0,1,2:T(8,128)(2,1)S(1)}, u32[]{:S(2)}, u32[]{:S(2)}) %collective-permute-start.13) | collective-permute-done | bytes 4128 | tf_op jit(solution)/shard_map/ppermute | solution.py:19
  108.1 3.4 %collective-permute-start.15 = (bf16[64,1,130]{0,1,2:T(2,128)(2,1)S(1)}, bf16[64,1,130]{0,1,2:T(2,128)(2,1)S(1)}, u32[]{:S(2)}, u32[]{:S(2)}) collective-permute-start(bf16[64,1,130]{0,1,2:T(2,128)(2,1)S(1)} %get-tuple-element.16), channel_id=1, source_target_pairs={{1,0},{2,1},{3,2},{4,3},{5,4},{6,5},{7,6},{9,8},{10,9},{11,10},{12... | collective-permute-start | bytes 49928 | tf_op jit(solution)/shard_map/ppermute | solution.py:19
  111.8 3.5 %collective-permute-done.15 = bf16[64,1,130]{0,1,2:T(2,128)(2,1)S(1)} collective-permute-done((bf16[64,1,130]{0,1,2:T(2,128)(2,1)S(1)}, bf16[64,1,130]{0,1,2:T(2,128)(2,1)S(1)}, u32[]{:S(2)}, u32[]{:S(2)}) %collective-permute-start.15) | collective-permute-done | bytes 16672 | tf_op jit(solution)/shard_map/ppermute | solution.py:19
  122.9 3.6 %collective-permute-start.16 = (bf16[32,32,1]{0,1,2:T(8,128)(2,1)S(1)}, bf16[32,32,1]{0,1,2:T(8,128)(2,1)S(1)}, u32[]{:S(2)}, u32[]{:S(2)}) collective-permute-start(bf16[32,32,1]{0,1,2:T(8,128)(2,1)S(1)} %get-tuple-element.27), channel_id=1, source_target_pairs={{0,8},{8,16},{16,24},{24,32},{32,40},{40,48},{48,56},{56,64},{64,7... | collective-permute-start | bytes 6152 | tf_op jit(solution)/shard_map/ppermute | solution.py:16
  136.4 3.4 %collective-permute-start.19 = (bf16[32,1,130]{0,1,2:T(2,128)(2,1)S(1)}, bf16[32,1,130]{0,1,2:T(2,128)(2,1)S(1)}, u32[]{:S(2)}, u32[]{:S(2)}) collective-permute-start(bf16[32,1,130]{0,1,2:T(2,128)(2,1)S(1)} %get-tuple-element.14), channel_id=1, source_target_pairs={{1,0},{2,1},{3,2},{4,3},{5,4},{6,5},{7,6},{9,8},{10,9},{11,10},{12... | collective-permute-start | bytes 24968 | tf_op jit(solution)/shard_map/ppermute | solution.py:19
  147.4 6.5 %collective-permute-start.20 = (bf16[32,32,1]{0,1,2:T(8,128)(2,1)S(1)}, bf16[32,32,1]{0,1,2:T(8,128)(2,1)S(1)}, u32[]{:S(2)}, u32[]{:S(2)}) collective-permute-start(bf16[32,32,1]{0,1,2:T(8,128)(2,1)S(1)} %get-tuple-element.25), channel_id=1, source_target_pairs={{0,8},{8,16},{16,24},{24,32},{32,40},{40,48},{48,56},{56,64},{64,7... | collective-permute-start | bytes 6152 | tf_op jit(solution)/shard_map/ppermute | solution.py:16
  162.1 3.4 %collective-permute-start.23 = (bf16[32,1,130]{0,1,2:T(2,128)(2,1)S(1)}, bf16[32,1,130]{0,1,2:T(2,128)(2,1)S(1)}, u32[]{:S(2)}, u32[]{:S(2)}) collective-permute-start(bf16[32,1,130]{0,1,2:T(2,128)(2,1)S(1)} %get-tuple-element.12), channel_id=1, source_target_pairs={{1,0},{2,1},{3,2},{4,3},{5,4},{6,5},{7,6},{9,8},{10,9},{11,10},{12... | collective-permute-start | bytes 24968 | tf_op jit(solution)/shard_map/ppermute | solution.py:19
  173.3 5.5 %collective-permute-start.24 = (bf16[32,32,1]{0,1,2:T(8,128)(2,1)S(1)}, bf16[32,32,1]{0,1,2:T(8,128)(2,1)S(1)}, u32[]{:S(2)}, u32[]{:S(2)}) collective-permute-start(bf16[32,32,1]{0,1,2:T(8,128)(2,1)S(1)} %get-tuple-element.23), channel_id=1, source_target_pairs={{0,8},{8,16},{16,24},{24,32},{32,40},{40,48},{48,56},{56,64},{64,7... | collective-permute-start | bytes 6152 | tf_op jit(solution)/shard_map/ppermute | solution.py:16
  187.5 3.3 %collective-permute-start.27 = (bf16[32,1,130]{0,1,2:T(2,128)(2,1)S(1)}, bf16[32,1,130]{0,1,2:T(2,128)(2,1)S(1)}, u32[]{:S(2)}, u32[]{:S(2)}) collective-permute-start(bf16[32,1,130]{0,1,2:T(2,128)(2,1)S(1)} %get-tuple-element.10), channel_id=1, source_target_pairs={{1,0},{2,1},{3,2},{4,3},{5,4},{6,5},{7,6},{9,8},{10,9},{11,10},{12... | collective-permute-start | bytes 24968 | tf_op jit(solution)/shard_map/ppermute | solution.py:19
  198.8 4.0 %collective-permute-start.28 = (bf16[32,32,1]{0,1,2:T(8,128)(2,1)S(1)}, bf16[32,32,1]{0,1,2:T(8,128)(2,1)S(1)}, u32[]{:S(2)}, u32[]{:S(2)}) collective-permute-start(bf16[32,32,1]{0,1,2:T(8,128)(2,1)S(1)} %get-tuple-element.21), channel_id=1, source_target_pairs={{0,8},{8,16},{16,24},{24,32},{32,40},{40,48},{48,56},{56,64},{64,7... | collective-permute-start | bytes 6152 | tf_op jit(solution)/shard_map/ppermute | solution.py:16
  211.8 3.5 %collective-permute-start.31 = (bf16[32,1,130]{0,1,2:T(2,128)(2,1)S(1)}, bf16[32,1,130]{0,1,2:T(2,128)(2,1)S(1)}, u32[]{:S(2)}, u32[]{:S(2)}) collective-permute-start(bf16[32,1,130]{0,1,2:T(2,128)(2,1)S(1)} %get-tuple-element.8), channel_id=1, source_target_pairs={{1,0},{2,1},{3,2},{4,3},{5,4},{6,5},{7,6},{9,8},{10,9},{11,10},{12... | collective-permute-start | bytes 24968 | tf_op jit(solution)/shard_map/ppermute | solution.py:19
  223.4 3.8 %collective-permute-start.32 = (bf16[64,32,1]{0,1,2:T(8,128)(2,1)S(1)}, bf16[64,32,1]{0,1,2:T(8,128)(2,1)S(1)}, u32[]{:S(2)}, u32[]{:S(2)}) collective-permute-start(bf16[64,32,1]{0,1,2:T(8,128)(2,1)S(1)} %get-tuple-element.19), channel_id=1, source_target_pairs={{0,8},{8,16},{16,24},{24,32},{32,40},{40,48},{48,56},{56,64},{64,7... | collective-permute-start | bytes 12296 | tf_op jit(solution)/shard_map/ppermute | solution.py:16
  229.1 4.5 %collective-permute-done.33 = bf16[64,32,1]{0,1,2:T(8,128)(2,1)S(1)} collective-permute-done((bf16[64,32,1]{0,1,2:T(8,128)(2,1)S(1)}, bf16[64,32,1]{0,1,2:T(8,128)(2,1)S(1)}, u32[]{:S(2)}, u32[]{:S(2)}) %collective-permute-start.33) | collective-permute-done | bytes 4128 | tf_op jit(solution)/shard_map/ppermute | solution.py:19
  239.2 4.1 %collective-permute-done.35 = bf16[64,1,130]{0,1,2:T(2,128)(2,1)S(1)} collective-permute-done((bf16[64,1,130]{0,1,2:T(2,128)(2,1)S(1)}, bf16[64,1,130]{0,1,2:T(2,128)(2,1)S(1)}, u32[]{:S(2)}, u32[]{:S(2)}) %collective-permute-start.35) | collective-permute-done | bytes 16672 | tf_op jit(solution)/shard_map/ppermute | solution.py:19
  245.1 4.1 %convolution_select_fusion = f32[32,8,17,12]{3,1,2,0:T(8,128)} fusion(bf16[3,3,12,64]{3,2,1,0:T(8,128)(2,1)S(1)} %bitcast.227, bf16[64,34,1,7,2]{0,3,4,1,2:T(8,128)(2,1)S(1)} %slice.260, bf16[64,34,1,8,17]{0,3,4,1,2:T(8,128)(2,1)S(1)} %copy.276, pred[8,17]{0,1:T(8,128)(4,1)S(1)} %copy-done.10), kind=kOutput, calls=%fused_computation.33 | convolution fusion | flops 62198784 | bytes 875656 | tf_op jit(solution)/shard_map/conv_general_dilated | solution.py:30
  249.2 3.3 %copy.277 = f32[32,8,17,12]{2,1,0,3:T(8,128)S(1)} copy(f32[32,8,17,12]{3,1,2,0:T(8,128)} %convolution_select_fusion) | data formatting | bytes 417792 | tf_op jit(solution)/shard_map/conv_general_dilated | solution.py:30
  253.0 6.8 %copy.278 = f32[3,32,2,128,2]{4,3,2,1,0:T(8,128)} copy(f32[3,32,2,128,2]{3,1,4,2,0:T(8,128)S(1)} %bitcast.212) | data formatting | bytes 393216 | tf_op jit(solution)/shard_map/transpose | solution.py:104
  259.8 9.9 %reshape_reshape.3 = f32[3,64,1,256]{3,1,0,2:T(8,128)S(1)} reshape(f32[3,32,2,128,2]{4,3,2,1,0:T(8,128)} %copy.278) | data formatting | bytes 393216 | tf_op jit(solution)/shard_map/reshape;reshape | solution.py:106
  269.8 46.1 %all_to_all.18 = f32[64,1,3,256]{3,1,2,0:T(1,128)S(1)} all-to-all(f32[64,1,3,256]{3,1,2,0:T(1,128)S(1)} %copy.279), channel_id=1, replica_groups=mesh['col'=64,'row'=8] {'col'}, dimensions={0} | all-to-all | bytes 393216 | tf_op jit(solution)/shard_map/all_to_all | solution.py:107
  (171 shorter events, 117.0 us)
Async XLA Ops:
  0.9 6.7 %collective-permute-start = (bf16[3,32,1]{2,1,0:T(8,128)(2,1)S(1)}, bf16[3,32,1]{2,1,0:T(8,128)(2,1)S(1)}, u32[]{:S(2)}, u32[]{:S(2)}) collective-permute-start(bf16[3,32,1]{2,1,0:T(8,128)(2,1)S(1)} %get-tuple-element.48), channel_id=1, source_target_pairs={{0,8},{8,16},{16,24},{24,32},{32,40},{40,48},{48,56},{56,64},{64,7... | collective-permute-start | bytes 584 | tf_op jit(solution)/shard_map/ppermute | solution.py:16
  5.7 6.0 %collective-permute-start.1 = (bf16[3,32,1]{2,1,0:T(8,128)(2,1)S(1)}, bf16[3,32,1]{2,1,0:T(8,128)(2,1)S(1)}, u32[]{:S(2)}, u32[]{:S(2)}) collective-permute-start(bf16[3,32,1]{2,1,0:T(8,128)(2,1)S(1)} %get-tuple-element.49), channel_id=1, source_target_pairs={{8,0},{16,8},{24,16},{32,24},{40,32},{48,40},{56,48},{64,56},{72,6... | collective-permute-start | bytes 584 | tf_op jit(solution)/shard_map/ppermute | solution.py:19
  15.6 6.5 %collective-permute-start.3 = (bf16[3,1,130]{2,1,0:T(2,128)(2,1)S(1)}, bf16[3,1,130]{2,1,0:T(2,128)(2,1)S(1)}, u32[]{:S(2)}, u32[]{:S(2)}) collective-permute-start(bf16[3,1,130]{2,1,0:T(2,128)(2,1)S(1)} %get-tuple-element.45), channel_id=1, source_target_pairs={{1,0},{2,1},{3,2},{4,3},{5,4},{6,5},{7,6},{9,8},{10,9},{11,10},{12... | collective-permute-start | bytes 2348 | tf_op jit(solution)/shard_map/ppermute | solution.py:19
  30.8 6.1 %collective-permute-start.5 = (bf16[32,32,1]{0,1,2:T(8,128)(2,1)S(1)}, bf16[32,32,1]{0,1,2:T(8,128)(2,1)S(1)}, u32[]{:S(2)}, u32[]{:S(2)}) collective-permute-start(bf16[32,32,1]{0,1,2:T(8,128)(2,1)S(1)} %get-tuple-element.32), channel_id=1, source_target_pairs={{8,0},{16,8},{24,16},{32,24},{40,32},{48,40},{56,48},{64,56},{72,6... | collective-permute-start | bytes 6152 | tf_op jit(solution)/shard_map/ppermute | solution.py:19
  37.1 5.6 %collective-permute-start.6 = (bf16[32,1,130]{0,1,2:T(2,128)(2,1)S(1)}, bf16[32,1,130]{0,1,2:T(2,128)(2,1)S(1)}, u32[]{:S(2)}, u32[]{:S(2)}) collective-permute-start(bf16[32,1,130]{0,1,2:T(2,128)(2,1)S(1)} %get-tuple-element.17), channel_id=1, source_target_pairs={{0,1},{1,2},{2,3},{3,4},{4,5},{5,6},{6,7},{8,9},{9,10},{10,11},{11... | collective-permute-start | bytes 24968 | tf_op jit(solution)/shard_map/ppermute | solution.py:16
  39.0 7.1 %collective-permute-start.7 = (bf16[32,1,130]{0,1,2:T(2,128)(2,1)S(1)}, bf16[32,1,130]{0,1,2:T(2,128)(2,1)S(1)}, u32[]{:S(2)}, u32[]{:S(2)}) collective-permute-start(bf16[32,1,130]{0,1,2:T(2,128)(2,1)S(1)} %get-tuple-element.18), channel_id=1, source_target_pairs={{1,0},{2,1},{3,2},{4,3},{5,4},{6,5},{7,6},{9,8},{10,9},{11,10},{12... | collective-permute-start | bytes 24968 | tf_op jit(solution)/shard_map/ppermute | solution.py:19
  73.3 5.7 %collective-permute-start.8 = (bf16[3,32,1]{2,1,0:T(8,128)(2,1)S(1)}, bf16[3,32,1]{2,1,0:T(8,128)(2,1)S(1)}, u32[]{:S(2)}, u32[]{:S(2)}) collective-permute-start(bf16[3,32,1]{2,1,0:T(8,128)(2,1)S(1)} %get-tuple-element.46), channel_id=1, source_target_pairs={{0,8},{8,16},{16,24},{24,32},{32,40},{40,48},{48,56},{56,64},{64,7... | collective-permute-start | bytes 584 | tf_op jit(solution)/shard_map/ppermute | solution.py:16
  77.0 6.8 %collective-permute-start.9 = (bf16[3,32,1]{2,1,0:T(8,128)(2,1)S(1)}, bf16[3,32,1]{2,1,0:T(8,128)(2,1)S(1)}, u32[]{:S(2)}, u32[]{:S(2)}) collective-permute-start(bf16[3,32,1]{2,1,0:T(8,128)(2,1)S(1)} %get-tuple-element.47), channel_id=1, source_target_pairs={{8,0},{16,8},{24,16},{32,24},{40,32},{48,40},{56,48},{64,56},{72,6... | collective-permute-start | bytes 584 | tf_op jit(solution)/shard_map/ppermute | solution.py:19
  83.9 6.0 %collective-permute-start.10 = (bf16[3,1,130]{2,1,0:T(2,128)(2,1)S(1)}, bf16[3,1,130]{2,1,0:T(2,128)(2,1)S(1)}, u32[]{:S(2)}, u32[]{:S(2)}) collective-permute-start(bf16[3,1,130]{2,1,0:T(2,128)(2,1)S(1)} %get-tuple-element.42), channel_id=1, source_target_pairs={{0,1},{1,2},{2,3},{3,4},{4,5},{5,6},{6,7},{8,9},{9,10},{10,11},{11... | collective-permute-start | bytes 2348 | tf_op jit(solution)/shard_map/ppermute | solution.py:16
  85.8 6.5 %collective-permute-start.11 = (bf16[3,1,130]{2,1,0:T(2,128)(2,1)S(1)}, bf16[3,1,130]{2,1,0:T(2,128)(2,1)S(1)}, u32[]{:S(2)}, u32[]{:S(2)}) collective-permute-start(bf16[3,1,130]{2,1,0:T(2,128)(2,1)S(1)} %get-tuple-element.43), channel_id=1, source_target_pairs={{1,0},{2,1},{3,2},{4,3},{5,4},{6,5},{7,6},{9,8},{10,9},{11,10},{12... | collective-permute-start | bytes 2348 | tf_op jit(solution)/shard_map/ppermute | solution.py:19
  99.3 6.8 %collective-permute-start.13 = (bf16[64,32,1]{0,1,2:T(8,128)(2,1)S(1)}, bf16[64,32,1]{0,1,2:T(8,128)(2,1)S(1)}, u32[]{:S(2)}, u32[]{:S(2)}) collective-permute-start(bf16[64,32,1]{0,1,2:T(8,128)(2,1)S(1)} %get-tuple-element.30), channel_id=1, source_target_pairs={{8,0},{16,8},{24,16},{32,24},{40,32},{48,40},{56,48},{64,56},{72,6... | collective-permute-start | bytes 12296 | tf_op jit(solution)/shard_map/ppermute | solution.py:19
  106.2 5.5 %collective-permute-start.14 = (bf16[64,1,130]{0,1,2:T(2,128)(2,1)S(1)}, bf16[64,1,130]{0,1,2:T(2,128)(2,1)S(1)}, u32[]{:S(2)}, u32[]{:S(2)}) collective-permute-start(bf16[64,1,130]{0,1,2:T(2,128)(2,1)S(1)} %get-tuple-element.15), channel_id=1, source_target_pairs={{0,1},{1,2},{2,3},{3,4},{4,5},{5,6},{6,7},{8,9},{9,10},{10,11},{11... | collective-permute-start | bytes 49928 | tf_op jit(solution)/shard_map/ppermute | solution.py:16
  108.1 7.1 %collective-permute-start.15 = (bf16[64,1,130]{0,1,2:T(2,128)(2,1)S(1)}, bf16[64,1,130]{0,1,2:T(2,128)(2,1)S(1)}, u32[]{:S(2)}, u32[]{:S(2)}) collective-permute-start(bf16[64,1,130]{0,1,2:T(2,128)(2,1)S(1)} %get-tuple-element.16), channel_id=1, source_target_pairs={{1,0},{2,1},{3,2},{4,3},{5,4},{6,5},{7,6},{9,8},{10,9},{11,10},{12... | collective-permute-start | bytes 49928 | tf_op jit(solution)/shard_map/ppermute | solution.py:19
  122.9 11.4 %collective-permute-start.16 = (bf16[32,32,1]{0,1,2:T(8,128)(2,1)S(1)}, bf16[32,32,1]{0,1,2:T(8,128)(2,1)S(1)}, u32[]{:S(2)}, u32[]{:S(2)}) collective-permute-start(bf16[32,32,1]{0,1,2:T(8,128)(2,1)S(1)} %get-tuple-element.27), channel_id=1, source_target_pairs={{0,8},{8,16},{16,24},{24,32},{32,40},{40,48},{48,56},{56,64},{64,7... | collective-permute-start | bytes 6152 | tf_op jit(solution)/shard_map/ppermute | solution.py:16
  126.5 7.8 %collective-permute-start.17 = (bf16[32,32,1]{0,1,2:T(8,128)(2,1)S(1)}, bf16[32,32,1]{0,1,2:T(8,128)(2,1)S(1)}, u32[]{:S(2)}, u32[]{:S(2)}) collective-permute-start(bf16[32,32,1]{0,1,2:T(8,128)(2,1)S(1)} %get-tuple-element.28), channel_id=1, source_target_pairs={{8,0},{16,8},{24,16},{32,24},{40,32},{48,40},{56,48},{64,56},{72,6... | collective-permute-start | bytes 6152 | tf_op jit(solution)/shard_map/ppermute | solution.py:19
  134.5 8.1 %collective-permute-start.18 = (bf16[32,1,130]{0,1,2:T(2,128)(2,1)S(1)}, bf16[32,1,130]{0,1,2:T(2,128)(2,1)S(1)}, u32[]{:S(2)}, u32[]{:S(2)}) collective-permute-start(bf16[32,1,130]{0,1,2:T(2,128)(2,1)S(1)} %get-tuple-element.13), channel_id=1, source_target_pairs={{0,1},{1,2},{2,3},{3,4},{4,5},{5,6},{6,7},{8,9},{9,10},{10,11},{11... | collective-permute-start | bytes 24968 | tf_op jit(solution)/shard_map/ppermute | solution.py:16
  136.4 7.1 %collective-permute-start.19 = (bf16[32,1,130]{0,1,2:T(2,128)(2,1)S(1)}, bf16[32,1,130]{0,1,2:T(2,128)(2,1)S(1)}, u32[]{:S(2)}, u32[]{:S(2)}) collective-permute-start(bf16[32,1,130]{0,1,2:T(2,128)(2,1)S(1)} %get-tuple-element.14), channel_id=1, source_target_pairs={{1,0},{2,1},{3,2},{4,3},{5,4},{6,5},{7,6},{9,8},{10,9},{11,10},{12... | collective-permute-start | bytes 24968 | tf_op jit(solution)/shard_map/ppermute | solution.py:19
  147.4 10.2 %collective-permute-start.20 = (bf16[32,32,1]{0,1,2:T(8,128)(2,1)S(1)}, bf16[32,32,1]{0,1,2:T(8,128)(2,1)S(1)}, u32[]{:S(2)}, u32[]{:S(2)}) collective-permute-start(bf16[32,32,1]{0,1,2:T(8,128)(2,1)S(1)} %get-tuple-element.25), channel_id=1, source_target_pairs={{0,8},{8,16},{16,24},{24,32},{32,40},{40,48},{48,56},{56,64},{64,7... | collective-permute-start | bytes 6152 | tf_op jit(solution)/shard_map/ppermute | solution.py:16
  154.0 5.9 %collective-permute-start.21 = (bf16[32,32,1]{0,1,2:T(8,128)(2,1)S(1)}, bf16[32,32,1]{0,1,2:T(8,128)(2,1)S(1)}, u32[]{:S(2)}, u32[]{:S(2)}) collective-permute-start(bf16[32,32,1]{0,1,2:T(8,128)(2,1)S(1)} %get-tuple-element.26), channel_id=1, source_target_pairs={{8,0},{16,8},{24,16},{32,24},{40,32},{48,40},{56,48},{64,56},{72,6... | collective-permute-start | bytes 6152 | tf_op jit(solution)/shard_map/ppermute | solution.py:19
  160.0 7.2 %collective-permute-start.22 = (bf16[32,1,130]{0,1,2:T(2,128)(2,1)S(1)}, bf16[32,1,130]{0,1,2:T(2,128)(2,1)S(1)}, u32[]{:S(2)}, u32[]{:S(2)}) collective-permute-start(bf16[32,1,130]{0,1,2:T(2,128)(2,1)S(1)} %get-tuple-element.11), channel_id=1, source_target_pairs={{0,1},{1,2},{2,3},{3,4},{4,5},{5,6},{6,7},{8,9},{9,10},{10,11},{11... | collective-permute-start | bytes 24968 | tf_op jit(solution)/shard_map/ppermute | solution.py:16
  162.1 7.1 %collective-permute-start.23 = (bf16[32,1,130]{0,1,2:T(2,128)(2,1)S(1)}, bf16[32,1,130]{0,1,2:T(2,128)(2,1)S(1)}, u32[]{:S(2)}, u32[]{:S(2)}) collective-permute-start(bf16[32,1,130]{0,1,2:T(2,128)(2,1)S(1)} %get-tuple-element.12), channel_id=1, source_target_pairs={{1,0},{2,1},{3,2},{4,3},{5,4},{6,5},{7,6},{9,8},{10,9},{11,10},{12... | collective-permute-start | bytes 24968 | tf_op jit(solution)/shard_map/ppermute | solution.py:19
  173.3 9.1 %collective-permute-start.24 = (bf16[32,32,1]{0,1,2:T(8,128)(2,1)S(1)}, bf16[32,32,1]{0,1,2:T(8,128)(2,1)S(1)}, u32[]{:S(2)}, u32[]{:S(2)}) collective-permute-start(bf16[32,32,1]{0,1,2:T(8,128)(2,1)S(1)} %get-tuple-element.23), channel_id=1, source_target_pairs={{0,8},{8,16},{16,24},{24,32},{32,40},{40,48},{48,56},{56,64},{64,7... | collective-permute-start | bytes 6152 | tf_op jit(solution)/shard_map/ppermute | solution.py:16
  178.8 6.3 %collective-permute-start.25 = (bf16[32,32,1]{0,1,2:T(8,128)(2,1)S(1)}, bf16[32,32,1]{0,1,2:T(8,128)(2,1)S(1)}, u32[]{:S(2)}, u32[]{:S(2)}) collective-permute-start(bf16[32,32,1]{0,1,2:T(8,128)(2,1)S(1)} %get-tuple-element.24), channel_id=1, source_target_pairs={{8,0},{16,8},{24,16},{32,24},{40,32},{48,40},{56,48},{64,56},{72,6... | collective-permute-start | bytes 6152 | tf_op jit(solution)/shard_map/ppermute | solution.py:19
  185.3 7.2 %collective-permute-start.26 = (bf16[32,1,130]{0,1,2:T(2,128)(2,1)S(1)}, bf16[32,1,130]{0,1,2:T(2,128)(2,1)S(1)}, u32[]{:S(2)}, u32[]{:S(2)}) collective-permute-start(bf16[32,1,130]{0,1,2:T(2,128)(2,1)S(1)} %get-tuple-element.9), channel_id=1, source_target_pairs={{0,1},{1,2},{2,3},{3,4},{4,5},{5,6},{6,7},{8,9},{9,10},{10,11},{11... | collective-permute-start | bytes 24968 | tf_op jit(solution)/shard_map/ppermute | solution.py:16
  187.5 7.1 %collective-permute-start.27 = (bf16[32,1,130]{0,1,2:T(2,128)(2,1)S(1)}, bf16[32,1,130]{0,1,2:T(2,128)(2,1)S(1)}, u32[]{:S(2)}, u32[]{:S(2)}) collective-permute-start(bf16[32,1,130]{0,1,2:T(2,128)(2,1)S(1)} %get-tuple-element.10), channel_id=1, source_target_pairs={{1,0},{2,1},{3,2},{4,3},{5,4},{6,5},{7,6},{9,8},{10,9},{11,10},{12... | collective-permute-start | bytes 24968 | tf_op jit(solution)/shard_map/ppermute | solution.py:19
  198.8 7.6 %collective-permute-start.28 = (bf16[32,32,1]{0,1,2:T(8,128)(2,1)S(1)}, bf16[32,32,1]{0,1,2:T(8,128)(2,1)S(1)}, u32[]{:S(2)}, u32[]{:S(2)}) collective-permute-start(bf16[32,32,1]{0,1,2:T(8,128)(2,1)S(1)} %get-tuple-element.21), channel_id=1, source_target_pairs={{0,8},{8,16},{16,24},{24,32},{32,40},{40,48},{48,56},{56,64},{64,7... | collective-permute-start | bytes 6152 | tf_op jit(solution)/shard_map/ppermute | solution.py:16
  202.8 6.6 %collective-permute-start.29 = (bf16[32,32,1]{0,1,2:T(8,128)(2,1)S(1)}, bf16[32,32,1]{0,1,2:T(8,128)(2,1)S(1)}, u32[]{:S(2)}, u32[]{:S(2)}) collective-permute-start(bf16[32,32,1]{0,1,2:T(8,128)(2,1)S(1)} %get-tuple-element.22), channel_id=1, source_target_pairs={{8,0},{16,8},{24,16},{32,24},{40,32},{48,40},{56,48},{64,56},{72,6... | collective-permute-start | bytes 6152 | tf_op jit(solution)/shard_map/ppermute | solution.py:19
  209.5 7.5 %collective-permute-start.30 = (bf16[32,1,130]{0,1,2:T(2,128)(2,1)S(1)}, bf16[32,1,130]{0,1,2:T(2,128)(2,1)S(1)}, u32[]{:S(2)}, u32[]{:S(2)}) collective-permute-start(bf16[32,1,130]{0,1,2:T(2,128)(2,1)S(1)} %get-tuple-element.7), channel_id=1, source_target_pairs={{0,1},{1,2},{2,3},{3,4},{4,5},{5,6},{6,7},{8,9},{9,10},{10,11},{11... | collective-permute-start | bytes 24968 | tf_op jit(solution)/shard_map/ppermute | solution.py:16
  211.8 7.1 %collective-permute-start.31 = (bf16[32,1,130]{0,1,2:T(2,128)(2,1)S(1)}, bf16[32,1,130]{0,1,2:T(2,128)(2,1)S(1)}, u32[]{:S(2)}, u32[]{:S(2)}) collective-permute-start(bf16[32,1,130]{0,1,2:T(2,128)(2,1)S(1)} %get-tuple-element.8), channel_id=1, source_target_pairs={{1,0},{2,1},{3,2},{4,3},{5,4},{6,5},{7,6},{9,8},{10,9},{11,10},{12... | collective-permute-start | bytes 24968 | tf_op jit(solution)/shard_map/ppermute | solution.py:19
  223.4 5.7 %collective-permute-start.32 = (bf16[64,32,1]{0,1,2:T(8,128)(2,1)S(1)}, bf16[64,32,1]{0,1,2:T(8,128)(2,1)S(1)}, u32[]{:S(2)}, u32[]{:S(2)}) collective-permute-start(bf16[64,32,1]{0,1,2:T(8,128)(2,1)S(1)} %get-tuple-element.19), channel_id=1, source_target_pairs={{0,8},{8,16},{16,24},{24,32},{32,40},{40,48},{48,56},{56,64},{64,7... | collective-permute-start | bytes 12296 | tf_op jit(solution)/shard_map/ppermute | solution.py:16
  227.1 6.5 %collective-permute-start.33 = (bf16[64,32,1]{0,1,2:T(8,128)(2,1)S(1)}, bf16[64,32,1]{0,1,2:T(8,128)(2,1)S(1)}, u32[]{:S(2)}, u32[]{:S(2)}) collective-permute-start(bf16[64,32,1]{0,1,2:T(8,128)(2,1)S(1)} %get-tuple-element.20), channel_id=1, source_target_pairs={{8,0},{16,8},{24,16},{32,24},{40,32},{48,40},{56,48},{64,56},{72,6... | collective-permute-start | bytes 12296 | tf_op jit(solution)/shard_map/ppermute | solution.py:19
  236.2 7.1 %collective-permute-start.35 = (bf16[64,1,130]{0,1,2:T(2,128)(2,1)S(1)}, bf16[64,1,130]{0,1,2:T(2,128)(2,1)S(1)}, u32[]{:S(2)}, u32[]{:S(2)}) collective-permute-start(bf16[64,1,130]{0,1,2:T(2,128)(2,1)S(1)} %get-tuple-element.6), channel_id=1, source_target_pairs={{1,0},{2,1},{3,2},{4,3},{5,4},{6,5},{7,6},{9,8},{10,9},{11,10},{12... | collective-permute-start | bytes 49928 | tf_op jit(solution)/shard_map/ppermute | solution.py:19
  (17 other events, 315.6 us)
where the time goes:
time: 322 us; the launch traced here: 317 us
  starting transfers between devices  106 us (33%)
  matrix products  66.1 us (21%)
  waiting for transfers between devices  54.9 us (17%)
  blocking collectives  46.1 us (14%)
  local copies, waits for them, and re-layouts  33.5 us (10%)
  other arithmetic  9.45 us (3%)
    conv_general_dilated x19, matrix products, conv_valid(): lax.conv_general_dilated(padded[None], kernel, (1, 1), 'VALID', dimension...  66.1 us
    ppermute x18, starting transfers between devices, padded_2(): lax.ppermute(lax.slice_in_dim(block, block.shape[dim] - width, None, axis...  58.4 us
    ppermute x18, waiting for transfers between devices, padded_2(): lax.ppermute(lax.slice_in_dim(block, 0, width, axis=dim), axis, backward)  54.9 us
    ppermute x18, starting transfers between devices, padded_2(): lax.ppermute(lax.slice_in_dim(block, 0, width, axis=dim), axis, backward)  47.1 us
    all_to_all x1, blocking collectives, on_device(): lax.all_to_all(outgoing, 'col', split_axis=0, concat_axis=3, tiled=True)  46.1 us
    another operation x1, local copies, waits for them, and re-layouts, on_device(): doubled.reshape(planes, col_count, band_rows, 2 * breadth)  9.85 us
    conv_general_dilated x27, local copies, waits for them, and re-layouts, conv_valid(): lax.conv_general_dilated(padded[None], kernel, (1, 1), 'VALID', dimension...  9.26 us
    transpose x1, local copies, waits for them, and re-layouts, on_device(): head_out.reshape(planes, 2, 2, height, breadth).transpose(0, 3, 1, 4, 2)  6.77 us
  transfers between devices with their start and end apart: 36, of which 17 were waited for; matrix products, arithmetic and copies ran while one was open for 6% of the time, Pallas kernels for 0%

commit v1 on v0

v1 whole, which is shorter than its diff:
```python
import jax
import jax.numpy as jnp
from jax import lax
from jax.experimental import pallas as pl
from jax.experimental.pallas import tpu as pltpu
from jax.sharding import PartitionSpec as P

BF = jnp.bfloat16
F32 = jnp.float32

STRIDE = 147
BASE = 128
PAIRS = 26
LANES = 4096
STEP = 256
HALO = 9
SOURCE = ((1, -1), (0, 0), (1, 0), (0, 1))


def shift_of(pair, tap):
    return pair * STRIDE + tap - 1


def tiles_of(layer):
    first = (layer + 1) // 2
    last = (50 - layer) // 2
    low = (BASE + first * STRIDE) // 128 * 128
    high = BASE + (last + 1) * STRIDE
    return range(low, high, STEP)


def iota(shape, dim):
    return lax.broadcasted_iota(jnp.int32, shape, dim)


def place_at(pair, phase):
    return 2 * pair + phase + 1


def picking(rows, depth, entries):
    return jnp.where(entries(iota((rows, depth), 0), iota((rows, depth), 1)), 1.0, 0.0).astype(BF)


def quotient(values, by):
    return lax.shift_right_arithmetic(values * (65536 // by + 1), 16)


def prep_kernel(
    loop_in, loop_out, first_conv, d1, d2, d3, d4, d5, head,
    w_in, w_out, w_first, w_f, w_1, w_2, w_3, w_4, w_head,
):
    for source, target in ((loop_in, w_in), (first_conv, w_first)):
        outs = source.shape[2]
        blank = jnp.zeros((1, outs), F32)
        flat = jnp.concatenate(
            [piece for t in range(9) for piece in (source[t].astype(F32), blank)], axis=0
        ).astype(BF)
        sides = []
        for p in range(2):

            def entries(m, k):
                group = lax.shift_right_arithmetic(m, 3)
                pair = quotient(group, 3)
                tap = group - 3 * pair
                down = 2 * pair - 1 + (lax.shift_right_arithmetic(m, 2) & 1) - p
                ok = (down >= 0) & (down <= 2) & ((m & 3) < 3)
                return ok & (k == (down * 3 + tap) * 4 + (m & 3))

            sides.append(jnp.dot(picking(72, 36, entries), flat, preferred_element_type=F32))
        target[...] = jnp.concatenate(sides, axis=1).T.astype(BF)
    blank = jnp.zeros((1, 32), F32)
    flat = jnp.concatenate(
        [piece for t in range(9) for piece in (loop_out[t].astype(F32), blank)], axis=0
    ).astype(BF)
    sides = []
    for q in range(2):

        def entries(m, k):
            group = lax.shift_right_arithmetic(m, 3)
            pair = quotient(group, 3)
            tap = group - 3 * pair
            down = 2 * pair - 1 + q - (lax.shift_right_arithmetic(m, 2) & 1)
            ok = (down >= 0) & (down <= 2) & ((m & 3) < 3)
            return ok & (k == (down * 3 + tap) * 4 + (m & 3))

        sides.append(jnp.dot(picking(72, 36, entries), flat, preferred_element_type=F32))
    w_out[...] = jnp.concatenate(sides, axis=1).astype(BF)
    blank = jnp.zeros((4, 64), F32)
    flat = jnp.concatenate(
        [piece for t in range(9) for piece in (head[t].astype(F32), blank)], axis=0
    ).astype(BF)
    sides = []
    for q in range(2):

        def entries(m, k):
            group = lax.shift_right_arithmetic(m, 5)
            pair = quotient(group, 3)
            tap = group - 3 * pair
            b = lax.shift_right_arithmetic(m, 4) & 1
            p = lax.shift_right_arithmetic(m, 3) & 1
            a = lax.shift_right_arithmetic(m, 2) & 1
            down = 2 * pair - 1 + q - p
            ok = (down >= 0) & (down <= 2) & ((m & 3) < 3)
            return ok & (k == (down * 3 + tap) * 16 + 4 * (m & 3) + 2 * a + b)

        sides.append(jnp.dot(picking(288, 144, entries), flat, preferred_element_type=F32))
    w_head[...] = jnp.concatenate(sides, axis=1).astype(BF)
    dense = (d1, d2, d3, d4, d5)
    for source, target in enumerate((w_f, w_1, w_2, w_3, w_4)):
        low = 0 if source == 0 else 32 + 32 * source
        ins = 64 if source == 0 else 32
        row = 0
        for weight in dense[source:]:
            outs = weight.shape[1]
            taps = [weight[t, :, low : low + ins] for t in range(9)]
            none = jnp.zeros((outs, 3 * ins), BF)
            joined = jnp.concatenate(taps, axis=1)
            target[row : row + outs, :] = jnp.concatenate([joined, none], axis=1)
            target[row + outs : row + 2 * outs, :] = jnp.concatenate([none, joined], axis=1)
            row += 2 * outs


def run_prep(*weights):
    vmem = pl.BlockSpec(memory_space=pltpu.VMEM)
    shapes = ((64, 72), (72, 64), (128, 72), (384, 768), (320, 384), (256, 384), (192, 384), (128, 384), (288, 128))
    return pl.pallas_call(
        prep_kernel,
        out_shape=[jax.ShapeDtypeStruct(shape, BF) for shape in shapes],
        in_specs=[vmem] * 9,
        out_specs=[vmem] * 9,
        compiler_params=pltpu.CompilerParams(vmem_limit_bytes=8 << 20),
        cost_estimate=pl.CostEstimate(flops=20_000_000, bytes_accessed=3_000_000, transcendentals=0),
        name="weights",
    )(*weights)


def lrelu(values):
    return jnp.maximum(values, 0.2 * values)


def main_kernel(
    place, ext, above, below, w_in, w_out, w_first, w_f, w_1, w_2, w_3, w_4, w_head,
    y_ref, x0, mask, hid, fil, xf, x1, x2, x3, x4, xb, acc, zs, hs,
):
    row_at = place[0]
    col_at = place[1]
    seam = col_at == 0
    for ref in (x0, hid, fil, xf, x1, x2, x3, x4, xb, zs):
        ref[...] = jnp.zeros(ref.shape, ref.dtype)

    lane = iota((8, LANES), 1) - BASE
    pair = lax.shift_right_arithmetic(lane * 28533, 22)
    column = lane - pair * STRIDE
    gap = jnp.logical_and(seam, column == 18)
    for phase in range(2):
        row = 2 * pair + phase - 1 - HALO + 32 * row_at
        keep = jnp.logical_and(jnp.logical_and(row >= 0, row < 256), jnp.logical_not(gap))
        mask[phase] = jnp.where(keep, 1.0, 0.0)

    def masked(values, phase, start):
        rows = values.shape[0]
        inside = mask[phase, :, start : start + STEP]
        return (values.reshape(rows // 8, 8, STEP) * inside[None]).reshape(rows, STEP)

    def wide(ref, plane):
        return jnp.concatenate([ref[0, plane], ref[1, plane]], axis=1)

    stacked = jnp.concatenate(
        [wide(ref, plane) for plane in range(3) for ref in (above, ext, below)], axis=0
    )
    rows = 8 * PAIRS
    m_at = iota((rows, 288), 0)
    k_at = iota((rows, 288), 1)
    stored = 2 * lax.shift_right_arithmetic(m_at, 3) + (lax.shift_right_arithmetic(m_at, 2) & 1)
    plane_at = m_at & 3
    pick = (plane_at < 3) & (stored >= 1) & (stored <= 50) & (k_at == plane_at * 96 + stored + 22)
    ordered = jnp.dot(
        jnp.where(pick, 1.0, 0.0).astype(BF), stacked, preferred_element_type=F32
    ).astype(BF)
    i_at = iota((256, 256), 0) - 110
    o_at = iota((256, 256), 1)
    late = jnp.logical_and(seam, o_at >= 18)
    wanted = jnp.where(late, o_at - 1, o_at)
    valid = (o_at < STRIDE) & jnp.logical_not(jnp.logical_and(seam, o_at == 18))
    place_cols = jnp.where((i_at == wanted) & valid, 1.0, 0.0).astype(BF)
    laid = jnp.dot(ordered, place_cols, preferred_element_type=F32)
    for g in range(PAIRS):
        x0[:, BASE + g * STRIDE : BASE + (g + 1) * STRIDE] = laid[8 * g : 8 * g + 8, :STRIDE]

    shifts = [(pair, tap) for pair in (-1, 0, 1) for tap in range(3)]

    def narrow_columns(ref, start):
        pieces = [
            ref[:, start + shift_of(pair, tap) : start + shift_of(pair, tap) + STEP]
            for pair, tap in shifts
        ]
        return jnp.concatenate(pieces, axis=0).astype(BF)

    for start in tiles_of(1):
        values = lrelu(jnp.dot(w_in[...], narrow_columns(x0, start), preferred_element_type=F32))
        for phase in range(2):
            part = slice(32 * phase, 32 * phase + 32)
            hid[part, start : start + STEP] = masked(values[part], phase, start).astype(BF)
    for start in tiles_of(1):
        zs[:, start : start + STEP] = jnp.dot(
            w_out[...], hid[:, start : start + STEP], preferred_element_type=F32
        )
    sub = iota((8, STEP), 0)
    for start in tiles_of(2):
        values = x0[:, start : start + STEP]
        for at, (pair_, tap) in enumerate(shifts):
            off = start + shift_of(pair_, tap)
            values = values + zs[8 * at : 8 * at + 8, off : off + STEP]
        inside = jnp.where(
            sub < 4, mask[0, :, start : start + STEP], mask[1, :, start : start + STEP]
        )
        fil[:, start : start + STEP] = (values * inside).astype(BF).astype(F32)

    for start in tiles_of(3):
        values = jnp.dot(w_first[...], narrow_columns(fil, start), preferred_element_type=F32)
        for phase in range(2):
            part = slice(64 * phase, 64 * phase + 64)
            xf[part, start : start + STEP] = masked(values[part], phase, start).astype(BF)

    def columns(ref, start):
        count = ref.shape[0] // 2
        pieces = []
        for phase, pair_ in SOURCE:
            for tap in range(3):
                off = start + shift_of(pair_, tap)
                pieces.append(ref[count * phase : count * (phase + 1), off : off + STEP])
        return jnp.concatenate(pieces, axis=0)

    for layer, (ref, weight, target) in enumerate(
        ((xf, w_f, x1), (x1, w_1, x2), (x2, w_2, x3), (x3, w_3, x4), (x4, w_4, xb))
    ):
        low = 64 * layer
        for start in tiles_of(4 + layer):
            span = slice(start, start + STEP)
            values = jnp.dot(weight[...], columns(ref, start), preferred_element_type=F32)
            if layer > 0:
                values = values + acc[low:, span]
            if layer < 4:
                acc[low + 64 :, span] = values[64:]
                values = lrelu(values[:64])
                count = 32
            else:
                values = xf[:, span].astype(F32) + 0.2 * values
                count = 64
            for phase in range(2):
                part = slice(count * phase, count * (phase + 1))
                target[part, span] = masked(values[part], phase, start).astype(BF)

    for start in tiles_of(8):
        hs[:, start : start + STEP] = jnp.dot(
            w_head[...], xb[:, start : start + STEP], preferred_element_type=F32
        )
    rows_out = []
    for g in range(5, 21):
        low = BASE + g * STRIDE
        values = None
        for at, (pair_, tap) in enumerate(shifts):
            off = low + shift_of(pair_, tap)
            term = hs[32 * at : 32 * at + 32, off : off + STEP]
            values = term if values is None else values + term
        rows_out.append(values.astype(BF))
    even = jnp.concatenate([values[:16] for values in rows_out], axis=0)
    odd = jnp.concatenate([values[16:] for values in rows_out], axis=0)
    k_at = iota((256, 256), 0)
    n_at = iota((256, 256), 1)
    cell = lax.shift_right_arithmetic(n_at, 1) + HALO
    cell = jnp.where(jnp.logical_and(seam, cell >= 18), cell + 1, cell)
    spread = [
        jnp.where((k_at == cell) & ((n_at & 1) == b), 1.0, 0.0).astype(BF) for b in range(2)
    ]
    result = jnp.dot(even, spread[0], preferred_element_type=F32) + jnp.dot(
        odd, spread[1], preferred_element_type=F32
    )
    first = result[:, :128].reshape(32, 8, 128)
    second = result[:, 128:].reshape(32, 8, 128)
    top = iota((32, 8, 128), 1) < 4
    even_rows = jnp.where(top, first, pltpu.roll(second, 4, 1)).astype(BF)
    odd_rows = jnp.where(top, pltpu.roll(first, 4, 1), second).astype(BF)
    for i in range(32):
        y_ref[2 * i] = even_rows[i]
        y_ref[2 * i + 1] = odd_rows[i]


def run_main(place, ext, above, below, weights):
    vmem = pl.BlockSpec(memory_space=pltpu.VMEM)
    return pl.pallas_call(
        main_kernel,
        out_shape=jax.ShapeDtypeStruct((64, 8, 128), BF),
        in_specs=[pl.BlockSpec(memory_space=pltpu.SMEM)] + [vmem] * 12,
        out_specs=vmem,
        scratch_shapes=[
            pltpu.VMEM((8, LANES), F32),
            pltpu.VMEM((2, 8, LANES), F32),
            pltpu.VMEM((64, LANES), BF),
            pltpu.VMEM((8, LANES), F32),
            pltpu.VMEM((128, LANES), BF),
            pltpu.VMEM((64, LANES), BF),
            pltpu.VMEM((64, LANES), BF),
            pltpu.VMEM((64, LANES), BF),
            pltpu.VMEM((64, LANES), BF),
            pltpu.VMEM((128, LANES), BF),
            pltpu.VMEM((384, LANES), F32),
            pltpu.VMEM((72, LANES), F32),
            pltpu.VMEM((288, LANES), F32),
        ],
        compiler_params=pltpu.CompilerParams(vmem_limit_bytes=48 << 20),
        cost_estimate=pl.CostEstimate(
            flops=2_000_000_000, bytes_accessed=4_000_000, transcendentals=0
        ),
        name="network",
    )(place, ext, above, below, *weights)


def rows_kernel(z_ref, o_ref):
    lane = iota((4, 128), 1)
    head = lane < 110

    def halves(source):
        turned = pltpu.roll(z_ref[source].astype(F32), 110, 1)
        return turned[:4], turned[4:]

    count = z_ref.shape[0]
    first, second = halves(0)
    opening = first
    for source in range(count):
        following = halves(source + 1) if source + 1 < count else (opening, None)
        at = 256 * source
        early = jnp.where(head, first, second)
        later = jnp.where(head, second, following[0])
        for plane in range(3):
            o_ref[plane, :, at : at + 128] = early[plane : plane + 1]
            o_ref[plane, :, at + 128 : at + 256] = later[plane : plane + 1]
        first, second = following


def run_rows(received):
    vmem = pl.BlockSpec(memory_space=pltpu.VMEM)
    return pl.pallas_call(
        rows_kernel,
        out_shape=jax.ShapeDtypeStruct((3, 1, 256 * received.shape[0]), F32),
        in_specs=[vmem],
        out_specs=vmem,
        compiler_params=pltpu.CompilerParams(vmem_limit_bytes=8 << 20),
        name="rows",
    )(received)


def on_device(decoded, loop_in, loop_out, first_conv, d1, d2, d3, d4, d5, head_conv):
    cols = lax.axis_size("col")
    rows = lax.axis_size("row")
    weights = run_prep(
        loop_in.transpose(0, 2, 1), loop_out, first_conv.transpose(0, 2, 1),
        d1, d2, d3, d4, d5, head_conv,
    )
    left = lax.ppermute(decoded, "col", [(i, (i + 1) % cols) for i in range(cols)])
    ext = jnp.stack([left, decoded])
    above = lax.ppermute(ext, "row", [(i, i + 1) for i in range(rows - 1)])
    below = lax.ppermute(ext, "row", [(i + 1, i) for i in range(rows - 1)])
    place = jnp.stack([lax.axis_index("row"), lax.axis_index("col")]).astype(jnp.int32)
    sent = run_main(place, ext, above, below, weights)
    received = lax.all_to_all(sent, "col", split_axis=0, concat_axis=0, tiled=True)
    return run_rows(received).transpose(1, 0, 2)[None]


def solution(mesh):
    in_specs = (P(None, "row", "col"), P(), P(), P(), P(), P(), P(), P(), P(), P())
    out_specs = P("row", "col", None, None)
    return jax.shard_map(
        on_device, mesh=mesh, in_specs=in_specs, out_specs=out_specs, check_vma=False
    )
```

time: 322 us -> 68.9 us (0.21); the launches traced: 317 us -> 68.4 us
  starting transfers between devices: 106 us -> 12.4 us
  matrix products: 66.1 us -> 0 us
  waiting for transfers between devices: 54.9 us -> 1.14 us
  local copies, waits for them, and re-layouts: 33.5 us -> 5.04 us
  Pallas kernels: 0 us -> 17.1 us
  blocking collectives: 46.1 us -> 31.7 us
  other arithmetic: 9.45 us -> 0.83 us
    ppermute x36 -> x3, starting transfers between devices: 106 us -> 12.4 us  [the longest x1 4.94 us: on_device(): above = lax.ppermute(ext, 'row', [(i, i + 1) for i in range(rows - 1)])]
    conv_general_dilated x19 -> x0, matrix products: 66.1 us -> none  [conv_valid(): lax.conv_general_dilated(padded[None], kernel, (1, 1), 'VALID', dimension...]
    ppermute x36 -> x3, waiting for transfers between devices: 54.9 us -> 1.14 us  [the longest x1 1.13 us: on_device(): lax.ppermute(decoded, 'col', [(i, (i + 1) % cols) for i in range(cols)])]
    pallas_call x0 -> x3, Pallas kernels: none -> 17.1 us  [the longest x1 15 us: run_main(): pl.pallas_call(main_kernel, out_shape=jax.ShapeDtypeStruct((64, 8, 128),...]
    all_to_all x1, blocking collectives: 46.1 us -> 31.7 us  [on_device(): lax.all_to_all(sent, 'col', split_axis=0, concat_axis=0, tiled=True)]
    another operation x1 -> x0, local copies, waits for them, and re-layouts: 9.85 us -> none  [on_device(): doubled.reshape(planes, col_count, band_rows, 2 * breadth)]
    conv_general_dilated x27 -> x0, local copies, waits for them, and re-layouts: 9.26 us -> none  [conv_valid(): lax.conv_general_dilated(padded[None], kernel, (1, 1), 'VALID', dimension...]
    transpose x2 -> x0, local copies, waits for them, and re-layouts: 6.97 us -> none  [the longest x1 6.77 us: on_device(): head_out.reshape(planes, 2, 2, height, breadth).transpose(0, 3, 1, 4, 2)]
  transfers between devices with their start and end apart: 36 -> 3, of which waited for: 17 -> 1; matrix products, arithmetic and copies ran while one was open for 6% -> 0% of each run, Pallas kernels for 0% -> 2%
where the time goes in v1:
time: 68.9 us; the launch traced here: 68.4 us
  blocking collectives  31.7 us (46%)
  Pallas kernels  17.1 us (25%)
  starting transfers between devices  12.4 us (18%)
  local copies, waits for them, and re-layouts  5.04 us (7%)
  waiting for transfers between devices  1.14 us (2%)
  other arithmetic  0.83 us (1%)
    all_to_all x1, blocking collectives, on_device(): lax.all_to_all(sent, 'col', split_axis=0, concat_axis=0, tiled=True)  31.7 us
    pallas_call x1, Pallas kernels, run_main(): pl.pallas_call(main_kernel, out_shape=jax.ShapeDtypeStruct((64, 8, 128),...  15 us
    unnamed x18, local copies, waits for them, and re-layouts  5.04 us
    ppermute x1, starting transfers between devices, on_device(): above = lax.ppermute(ext, 'row', [(i, i + 1) for i in range(rows - 1)])  4.94 us
    ppermute x1, starting transfers between devices, on_device(): lax.ppermute(decoded, 'col', [(i, (i + 1) % cols) for i in range(cols)])  4.9 us
    ppermute x1, starting transfers between devices, on_device(): below = lax.ppermute(ext, 'row', [(i + 1, i) for i in range(rows - 1)])  2.58 us
  transfers between devices with their start and end apart: 3, of which 1 were waited for; matrix products, arithmetic and copies ran while one was open for 0% of the time, Pallas kernels for 2%

profile of v1, /device:TPU:7, one launch (start us, length us, event | category | flops | bytes accessed | tf_op | source)
XLA Modules:
  0.0 68.4 jit_solution(5517729120615306027)
XLA Ops:
  0.0 0.0 copy-start.2
  0.0 4.9 %collective-permute-start = (bf16[3,32,128]{2,1,0:T(8,128)(2,1)}, bf16[3,32,128]{2,1,0:T(8,128)(2,1)S(1)}, u32[]{:S(2)}, u32[]{:S(2)}) collective-permute-start(bf16[3,32,128]{2,1,0:T(8,128)(2,1)} %param.10), channel_id=1, source_target_pairs={{0,8},{8,16},{16,24},{24,32},{32,40},{40,48},{48,56},{56,64},{64,7... | collective-permute-start | bytes 73736 | tf_op jit(solution)/shard_map/ppermute | solution.py:360
  4.9 1.1 %collective-permute-done = bf16[3,32,128]{2,1,0:T(8,128)(2,1)S(1)} collective-permute-done((bf16[3,32,128]{2,1,0:T(8,128)(2,1)}, bf16[3,32,128]{2,1,0:T(8,128)(2,1)S(1)}, u32[]{:S(2)}, u32[]{:S(2)}) %collective-permute-start) | collective-permute-done | bytes 24608 | tf_op jit(solution)/shard_map/ppermute | solution.py:360
  6.0 0.0 copy-start.5
  6.0 0.7 %pad_maximum_fusion.ext = bf16[2,3,32,128]{3,2,1,0:T(8,128)(2,1)S(1)} fusion(bf16[1,3,32,128]{3,2,1,0:T(8,128)(2,1)} %bitcast.11, bf16[1,3,32,128]{3,2,1,0:T(8,128)(2,1)S(1)} %bitcast.12), kind=kLoop, calls=%fused_computation | loop fusion | flops 24576 | bytes 98304 | tf_op jit(solution)/shard_map/stack | solution.py:361
  6.8 0.0 copy-start.6
  6.8 2.6 %collective-permute-start.2 = (bf16[2,3,32,128]{3,2,1,0:T(8,128)(2,1)S(1)}, bf16[2,3,32,128]{3,2,1,0:T(8,128)(2,1)S(1)}, u32[]{:S(2)}, u32[]{:S(2)}) collective-permute-start(bf16[2,3,32,128]{3,2,1,0:T(8,128)(2,1)S(1)} %pad_maximum_fusion.ext), channel_id=1, source_target_pairs={{1,0},{2,1},{3,2},{4,3},{5,4},{6,5},{7,6},{9,8},{10,9},{11,10},{12... | collective-permute-start | bytes 147464 | tf_op jit(solution)/shard_map/ppermute | solution.py:363
  9.4 4.9 %collective-permute-start.1 = (bf16[2,3,32,128]{3,2,1,0:T(8,128)(2,1)S(1)}, bf16[2,3,32,128]{3,2,1,0:T(8,128)(2,1)S(1)}, u32[]{:S(2)}, u32[]{:S(2)}) collective-permute-start(bf16[2,3,32,128]{3,2,1,0:T(8,128)(2,1)S(1)} %pad_maximum_fusion.ext), channel_id=1, source_target_pairs={{0,1},{1,2},{2,3},{3,4},{4,5},{5,6},{6,7},{8,9},{9,10},{10,11},{11... | collective-permute-start | bytes 147464 | tf_op jit(solution)/shard_map/ppermute | solution.py:362
  14.3 0.1 pad_add_fusion.place
  14.4 0.0 copy-done.2
  14.4 0.0 copy-done.5
  14.4 0.0 copy-done.6
  14.4 0.0 copy-start
  14.4 1.0 %copy-done = bf16[9,64,192]{2,1,0:T(8,128)(2,1)S(1)} copy-done((bf16[9,64,192]{2,1,0:T(8,128)(2,1)S(1)}, bf16[9,64,192]{2,1,0:T(8,128)(2,1)}, u32[]{:S(2)}) %copy-start) | copy-done | bytes 221208
  15.4 0.0 copy-start.1
  15.4 0.9 %copy-done.1 = bf16[9,32,160]{2,1,0:T(8,128)(2,1)S(1)} copy-done((bf16[9,32,160]{2,1,0:T(8,128)(2,1)S(1)}, bf16[9,32,160]{2,1,0:T(8,128)(2,1)}, u32[]{:S(2)}) %copy-start.1) | copy-done | bytes 92184
  16.3 0.0 copy-start.3
  16.3 0.9 %copy-done.3 = bf16[9,32,96]{2,1,0:T(8,128)(2,1)S(1)} copy-done((bf16[9,32,96]{2,1,0:T(8,128)(2,1)S(1)}, bf16[9,32,96]{2,1,0:T(8,128)(2,1)}, u32[]{:S(2)}) %copy-start.3) | copy-done | bytes 55320
  17.2 0.0 copy-start.4
  17.2 0.9 %copy-done.4 = bf16[9,32,128]{2,1,0:T(8,128)(2,1)S(1)} copy-done((bf16[9,32,128]{2,1,0:T(8,128)(2,1)S(1)}, bf16[9,32,128]{2,1,0:T(8,128)(2,1)}, u32[]{:S(2)}) %copy-start.4) | copy-done | bytes 73752
  18.1 0.0 copy-start.7
  18.1 0.7 %copy-done.7 = bf16[9,3,32]{2,1,0:T(4,128)(2,1)S(1)} copy-done((bf16[9,3,32]{2,1,0:T(4,128)(2,1)S(1)}, bf16[9,3,32]{2,1,0:T(4,128)(2,1)}, u32[]{:S(2)}) %copy-start.7) | copy-done | bytes 1752
  18.8 0.0 copy-start.8
  18.8 0.7 %copy-done.8 = bf16[9,64,3]{1,2,0:T(4,128)(2,1)S(1)} copy-done((bf16[9,64,3]{1,2,0:T(4,128)(2,1)S(1)}, bf16[9,64,3]{1,2,0:T(4,128)(2,1)}, u32[]{:S(2)}) %copy-start.8) | copy-done | bytes 3480
  19.5 1.3 %weights.1 = (bf16[64,72]{1,0:T(8,128)(2,1)S(1)}, bf16[72,64]{1,0:T(8,128)(2,1)S(1)}, bf16[128,72]{1,0:T(8,128)(2,1)S(1)}, bf16[384,768]{1,0:T(8,128)(2,1)S(1)},...) custom-call(bf16[9,3,32]{2,1,0:T(4,128)(2,1)S(1)} %bitcast.9, ...), custom_call_target="tpu_custom_call" | custom-call | flops 20000000 | bytes 3000000 | tf_op jit(solution)/shard_map/weights/pallas_call | solution.py:126
  20.7 0.0 collective-permute-done.2.below
  20.7 0.0 collective-permute-done.1.above
  20.7 15.0 %network.1 = bf16[64,8,128]{2,1,0:T(8,128)(2,1)S(1)} custom-call(s32[2]{0:T(128)S(1)} %pad_add_fusion.place, bf16[2,3,32,128]{3,2,1,0:T(8,128)(2,1)S(1)} %pad_maximum_fusion.ext, bf16[2,3,32,128]{3,2,1,0:T(8,128)(2,1)S(1)} %collective-permute-done.1.above, bf16[2,3,32,128]{3,2,1,0:T(8,128)(2,1)S(1)} %collective-permute-done.2.below, ...), custom_call_target="tpu_custom_call" | custom-call | flops 2000000000 | bytes 4000000 | tf_op jit(solution)/shard_map/network/pallas_call | solution.py:291
  35.7 31.7 %all_to_all.5.z_ref = bf16[64,8,128]{2,1,0:T(8,128)(2,1)S(1)} all-to-all(bf16[64,8,128]{2,1,0:T(8,128)(2,1)S(1)} %network.1), channel_id=1, replica_groups=mesh['col'=64,'row'=8] {'col'}, dimensions={0} | all-to-all | bytes 262144 | tf_op jit(solution)/shard_map/all_to_all | solution.py:366
  67.5 0.9 %rows.1 = f32[3,1,16384]{2,1,0:T(1,128)} custom-call(bf16[64,8,128]{2,1,0:T(8,128)(2,1)S(1)} %all_to_all.5.z_ref), custom_call_target="tpu_custom_call" | custom-call | tf_op jit(solution)/shard_map/rows/pallas_call | solution.py:343
Async XLA Ops:
  0.0 14.4 %copy-start.2 = (bf16[9,32,64]{2,1,0:T(8,128)(2,1)S(1)}, bf16[9,32,64]{2,1,0:T(8,128)(2,1)}, u32[]{:S(2)}) copy-start(bf16[9,32,64]{2,1,0:T(8,128)(2,1)} %d1.1) | copy-start | bytes 110596
  0.0 6.0 %collective-permute-start = (bf16[3,32,128]{2,1,0:T(8,128)(2,1)}, bf16[3,32,128]{2,1,0:T(8,128)(2,1)S(1)}, u32[]{:S(2)}, u32[]{:S(2)}) collective-permute-start(bf16[3,32,128]{2,1,0:T(8,128)(2,1)} %param.10), channel_id=1, source_target_pairs={{0,8},{8,16},{16,24},{24,32},{32,40},{40,48},{48,56},{56,64},{64,7... | collective-permute-start | bytes 73736 | tf_op jit(solution)/shard_map/ppermute | solution.py:360
  6.0 8.4 %copy-start.5 = (bf16[9,12,64]{2,1,0:T(8,128)(2,1)S(1)}, bf16[9,12,64]{2,1,0:T(8,128)(2,1)}, u32[]{:S(2)}) copy-start(bf16[9,12,64]{2,1,0:T(8,128)(2,1)} %head.1) | copy-start | bytes 41476
  6.8 7.6 %copy-start.6 = (bf16[9,32,3]{1,2,0:T(4,128)(2,1)S(1)}, bf16[9,32,3]{1,2,0:T(4,128)(2,1)}, u32[]{:S(2)}) copy-start(bf16[9,32,3]{1,2,0:T(4,128)(2,1)} %param.11) | copy-start | bytes 5188
  6.8 13.9 %collective-permute-start.2 = (bf16[2,3,32,128]{3,2,1,0:T(8,128)(2,1)S(1)}, bf16[2,3,32,128]{3,2,1,0:T(8,128)(2,1)S(1)}, u32[]{:S(2)}, u32[]{:S(2)}) collective-permute-start(bf16[2,3,32,128]{3,2,1,0:T(8,128)(2,1)S(1)} %pad_maximum_fusion.ext), channel_id=1, source_target_pairs={{1,0},{2,1},{3,2},{4,3},{5,4},{6,5},{7,6},{9,8},{10,9},{11,10},{12... | collective-permute-start | bytes 147464 | tf_op jit(solution)/shard_map/ppermute | solution.py:363
  9.4 11.4 %collective-permute-start.1 = (bf16[2,3,32,128]{3,2,1,0:T(8,128)(2,1)S(1)}, bf16[2,3,32,128]{3,2,1,0:T(8,128)(2,1)S(1)}, u32[]{:S(2)}, u32[]{:S(2)}) collective-permute-start(bf16[2,3,32,128]{3,2,1,0:T(8,128)(2,1)S(1)} %pad_maximum_fusion.ext), channel_id=1, source_target_pairs={{0,1},{1,2},{2,3},{3,4},{4,5},{5,6},{6,7},{8,9},{9,10},{10,11},{11... | collective-permute-start | bytes 147464 | tf_op jit(solution)/shard_map/ppermute | solution.py:362
  14.4 1.0 %copy-start = (bf16[9,64,192]{2,1,0:T(8,128)(2,1)S(1)}, bf16[9,64,192]{2,1,0:T(8,128)(2,1)}, u32[]{:S(2)}) copy-start(bf16[9,64,192]{2,1,0:T(8,128)(2,1)} %d5.1) | copy-start | bytes 663556
  15.4 0.9 %copy-start.1 = (bf16[9,32,160]{2,1,0:T(8,128)(2,1)S(1)}, bf16[9,32,160]{2,1,0:T(8,128)(2,1)}, u32[]{:S(2)}) copy-start(bf16[9,32,160]{2,1,0:T(8,128)(2,1)} %d4.1) | copy-start | bytes 276484
  16.3 0.9 %copy-start.3 = (bf16[9,32,96]{2,1,0:T(8,128)(2,1)S(1)}, bf16[9,32,96]{2,1,0:T(8,128)(2,1)}, u32[]{:S(2)}) copy-start(bf16[9,32,96]{2,1,0:T(8,128)(2,1)} %d2.1) | copy-start | bytes 165892
  17.2 0.9 %copy-start.4 = (bf16[9,32,128]{2,1,0:T(8,128)(2,1)S(1)}, bf16[9,32,128]{2,1,0:T(8,128)(2,1)}, u32[]{:S(2)}) copy-start(bf16[9,32,128]{2,1,0:T(8,128)(2,1)} %d3.1) | copy-start | bytes 221188
  18.1 0.7 %copy-start.7 = (bf16[9,3,32]{2,1,0:T(4,128)(2,1)S(1)}, bf16[9,3,32]{2,1,0:T(4,128)(2,1)}, u32[]{:S(2)}) copy-start(bf16[9,3,32]{2,1,0:T(4,128)(2,1)} %loop_out.1) | copy-start | bytes 5188
  18.8 0.7 %copy-start.8 = (bf16[9,64,3]{1,2,0:T(4,128)(2,1)S(1)}, bf16[9,64,3]{1,2,0:T(4,128)(2,1)}, u32[]{:S(2)}) copy-start(bf16[9,64,3]{1,2,0:T(4,128)(2,1)} %param.13) | copy-start | bytes 10372

commit v2 on v1

--- a/solution.py
+++ b/solution.py
@@ -12,7 +12,7 @@
 BASE = 128
 PAIRS = 26
 LANES = 4096
-STEP = 256
+STEP = 1024
 HALO = 9
 SOURCE = ((1, -1), (0, 0), (1, 0), (0, 1))
 
@@ -25,8 +25,8 @@
     first = (layer + 1) // 2
     last = (50 - layer) // 2
     low = (BASE + first * STRIDE) // 128 * 128
-    high = BASE + (last + 1) * STRIDE
-    return range(low, high, STEP)
+    high = -(-(BASE + (last + 1) * STRIDE) // 128) * 128
+    return [(start, min(STEP, high - start)) for start in range(low, high, STEP)]
 
 
 def iota(shape, dim):
@@ -45,10 +45,44 @@
     return lax.shift_right_arithmetic(values * (65536 // by + 1), 16)
 
 
-def prep_kernel(
-    loop_in, loop_out, first_conv, d1, d2, d3, d4, d5, head,
-    w_in, w_out, w_first, w_f, w_1, w_2, w_3, w_4, w_head,
-):
+def sections(pack):
+    return (
+        pack.at[896:960, 256:328],
+        pack.at[896:976, 384:448],
+        pack.at[896:1024, 128:200],
+        pack.at[0:384, 0:768],
+        pack.at[384:704, 0:384],
+        pack.at[384:640, 384:768],
+        pack.at[704:896, 0:384],
+        pack.at[704:832, 384:768],
+        pack.at[896:1184, 0:128],
+    )
+
+
+BANDS = ((896, 1184), (0, 384), (384, 704), (704, 896))
+
+
+def band_copies(source, target, done):
+    return [
+        pltpu.make_async_copy(source.at[low:high, :], target.at[low:high, :], done.at[i])
+        for i, (low, high) in enumerate(BANDS)
+    ]
+
+
+def prep_kernel(*refs):
+    given, whole, held, pack, arrived, left = refs[:9], refs[9], refs[10:19], *refs[19:22]
+    targets = sections(pack)
+    leaving = band_copies(pack, whole, left)
+    copies = [
+        pltpu.make_async_copy(source, target, arrived.at[i])
+        for i, (source, target) in enumerate(zip(given, held))
+    ]
+    for copy in copies:
+        copy.start()
+    for at in (0, 1, 2, 8):
+        copies[at].wait()
+    loop_in, loop_out, first_conv, d1, d2, d3, d4, d5, head = held
+    w_in, w_out, w_first, w_f, w_1, w_2, w_3, w_4, w_head = targets
     for source, target in ((loop_in, w_in), (first_conv, w_first)):
         outs = source.shape[2]
         blank = jnp.zeros((1, outs), F32)
@@ -83,7 +117,7 @@
             ok = (down >= 0) & (down <= 2) & ((m & 3) < 3)
             return ok & (k == (down * 3 + tap) * 4 + (m & 3))
 
-        sides.append(jnp.dot(picking(72, 36, entries), flat, preferred_element_type=F32))
+        sides.append(jnp.dot(picking(80, 36, entries), flat, preferred_element_type=F32))
     w_out[...] = jnp.concatenate(sides, axis=1).astype(BF)
     blank = jnp.zeros((4, 64), F32)
     flat = jnp.concatenate(
@@ -105,6 +139,9 @@
 
         sides.append(jnp.dot(picking(288, 144, entries), flat, preferred_element_type=F32))
     w_head[...] = jnp.concatenate(sides, axis=1).astype(BF)
+    leaving[0].start()
+    for at in range(3, 8):
+        copies[at].wait()
     dense = (d1, d2, d3, d4, d5)
     for source, target in enumerate((w_f, w_1, w_2, w_3, w_4)):
         low = 0 if source == 0 else 32 + 32 * source
@@ -118,17 +155,25 @@
             target[row : row + outs, :] = jnp.concatenate([joined, none], axis=1)
             target[row + outs : row + 2 * outs, :] = jnp.concatenate([none, joined], axis=1)
             row += 2 * outs
+        if source in (0, 2, 4):
+            leaving[1 + source // 2].start()
+    for copy in leaving:
+        copy.wait()
 
 
 def run_prep(*weights):
-    vmem = pl.BlockSpec(memory_space=pltpu.VMEM)
-    shapes = ((64, 72), (72, 64), (128, 72), (384, 768), (320, 384), (256, 384), (192, 384), (128, 384), (288, 128))
     return pl.pallas_call(
         prep_kernel,
-        out_shape=[jax.ShapeDtypeStruct(shape, BF) for shape in shapes],
-        in_specs=[vmem] * 9,
-        out_specs=[vmem] * 9,
-        compiler_params=pltpu.CompilerParams(vmem_limit_bytes=8 << 20),
+        out_shape=jax.ShapeDtypeStruct((1184, 768), BF),
+        in_specs=[pl.BlockSpec(memory_space=pltpu.HBM)] * 9,
+        out_specs=pl.BlockSpec(memory_space=pltpu.HBM),
+        scratch_shapes=[pltpu.VMEM(weight.shape, BF) for weight in weights]
+        + [
+            pltpu.VMEM((1184, 768), BF),
+            pltpu.SemaphoreType.DMA((9,)),
+            pltpu.SemaphoreType.DMA((4,)),
+        ],
+        compiler_params=pltpu.CompilerParams(vmem_limit_bytes=56 << 20),
         cost_estimate=pl.CostEstimate(flops=20_000_000, bytes_accessed=3_000_000, transcendentals=0),
         name="weights",
     )(*weights)
@@ -139,28 +184,29 @@
 
 
 def main_kernel(
-    place, ext, above, below, w_in, w_out, w_first, w_f, w_1, w_2, w_3, w_4, w_head,
-    y_ref, x0, mask, hid, fil, xf, x1, x2, x3, x4, xb, acc, zs, hs,
+    place, ext, above, below, pack, y_ref,
+    x0, mask, hid, fil, xf, x1, x2, x3, x4, xb, acc, zs, hs,
 ):
+    w_in, w_out, w_first, w_f, w_1, w_2, w_3, w_4, w_head = sections(pack)
     row_at = place[0]
     col_at = place[1]
-    seam = col_at == 0
     for ref in (x0, hid, fil, xf, x1, x2, x3, x4, xb, zs):
         ref[...] = jnp.zeros(ref.shape, ref.dtype)
 
     lane = iota((8, LANES), 1) - BASE
     pair = lax.shift_right_arithmetic(lane * 28533, 22)
     column = lane - pair * STRIDE
-    gap = jnp.logical_and(seam, column == 18)
+    first_column = jnp.where(col_at == 0, 2 * HALO, 0)
+    across = jnp.logical_and(column >= first_column, column < STRIDE - 1)
     for phase in range(2):
         row = 2 * pair + phase - 1 - HALO + 32 * row_at
-        keep = jnp.logical_and(jnp.logical_and(row >= 0, row < 256), jnp.logical_not(gap))
+        keep = jnp.logical_and(jnp.logical_and(row >= 0, row < 256), across)
         mask[phase] = jnp.where(keep, 1.0, 0.0)
 
     def masked(values, phase, start):
-        rows = values.shape[0]
-        inside = mask[phase, :, start : start + STEP]
-        return (values.reshape(rows // 8, 8, STEP) * inside[None]).reshape(rows, STEP)
+        rows, width = values.shape
+        inside = mask[phase, :, start : start + width]
+        return (values.reshape(rows // 8, 8, width) * inside[None]).reshape(rows, width)
 
     def wide(ref, plane):
         return jnp.concatenate([ref[0, plane], ref[1, plane]], axis=1)
@@ -179,65 +225,61 @@
     ).astype(BF)
     i_at = iota((256, 256), 0) - 110
     o_at = iota((256, 256), 1)
-    late = jnp.logical_and(seam, o_at >= 18)
-    wanted = jnp.where(late, o_at - 1, o_at)
-    valid = (o_at < STRIDE) & jnp.logical_not(jnp.logical_and(seam, o_at == 18))
-    place_cols = jnp.where((i_at == wanted) & valid, 1.0, 0.0).astype(BF)
+    place_cols = jnp.where(i_at == o_at, 1.0, 0.0).astype(BF)
     laid = jnp.dot(ordered, place_cols, preferred_element_type=F32)
     for g in range(PAIRS):
         x0[:, BASE + g * STRIDE : BASE + (g + 1) * STRIDE] = laid[8 * g : 8 * g + 8, :STRIDE]
 
     shifts = [(pair, tap) for pair in (-1, 0, 1) for tap in range(3)]
 
-    def narrow_columns(ref, start):
+    def narrow_columns(ref, start, width):
         pieces = [
-            ref[:, start + shift_of(pair, tap) : start + shift_of(pair, tap) + STEP]
+            ref[:, start + shift_of(pair, tap) : start + shift_of(pair, tap) + width]
             for pair, tap in shifts
         ]
         return jnp.concatenate(pieces, axis=0).astype(BF)
 
-    for start in tiles_of(1):
-        values = lrelu(jnp.dot(w_in[...], narrow_columns(x0, start), preferred_element_type=F32))
+    for start, width in tiles_of(1):
+        values = lrelu(jnp.dot(w_in[...], narrow_columns(x0, start, width), preferred_element_type=F32))
         for phase in range(2):
             part = slice(32 * phase, 32 * phase + 32)
-            hid[part, start : start + STEP] = masked(values[part], phase, start).astype(BF)
-    for start in tiles_of(1):
-        zs[:, start : start + STEP] = jnp.dot(
-            w_out[...], hid[:, start : start + STEP], preferred_element_type=F32
+            hid[part, start : start + width] = masked(values[part], phase, start).astype(BF)
+    for start, width in tiles_of(1):
+        zs[:, start : start + width] = jnp.dot(
+            w_out[...], hid[:, start : start + width], preferred_element_type=F32
         )
-    sub = iota((8, STEP), 0)
-    for start in tiles_of(2):
-        values = x0[:, start : start + STEP]
+    for start, width in tiles_of(2):
+        values = x0[:, start : start + width]
         for at, (pair_, tap) in enumerate(shifts):
             off = start + shift_of(pair_, tap)
-            values = values + zs[8 * at : 8 * at + 8, off : off + STEP]
+            values = values + zs[8 * at : 8 * at + 8, off : off + width]
         inside = jnp.where(
-            sub < 4, mask[0, :, start : start + STEP], mask[1, :, start : start + STEP]
+            iota((8, width), 0) < 4, mask[0, :, start : start + width], mask[1, :, start : start + width]
         )
-        fil[:, start : start + STEP] = (values * inside).astype(BF).astype(F32)
-
-    for start in tiles_of(3):
-        values = jnp.dot(w_first[...], narrow_columns(fil, start), preferred_element_type=F32)
+        fil[:, start : start + width] = (values * inside).astype(BF).astype(F32)
+
+    for start, width in tiles_of(3):
+        values = jnp.dot(w_first[...], narrow_columns(fil, start, width), preferred_element_type=F32)
         for phase in range(2):
             part = slice(64 * phase, 64 * phase + 64)
-            xf[part, start : start + STEP] = masked(values[part], phase, start).astype(BF)
-
-    def columns(ref, start):
+            xf[part, start : start + width] = masked(values[part], phase, start).astype(BF)
+
+    def columns(ref, start, width):
         count = ref.shape[0] // 2
         pieces = []
         for phase, pair_ in SOURCE:
             for tap in range(3):
                 off = start + shift_of(pair_, tap)
-                pieces.append(ref[count * phase : count * (phase + 1), off : off + STEP])
+                pieces.append(ref[count * phase : count * (phase + 1), off : off + width])
         return jnp.concatenate(pieces, axis=0)
 
     for layer, (ref, weight, target) in enumerate(
         ((xf, w_f, x1), (x1, w_1, x2), (x2, w_2, x3), (x3, w_3, x4), (x4, w_4, xb))
     ):
         low = 64 * layer
-        for start in tiles_of(4 + layer):
-            span = slice(start, start + STEP)
-            values = jnp.dot(weight[...], columns(ref, start), preferred_element_type=F32)
+        for start, width in tiles_of(4 + layer):
+            span = slice(start, start + width)
+            values = jnp.dot(weight[...], columns(ref, start, width), preferred_element_type=F32)
             if layer > 0:
                 values = values + acc[low:, span]
             if layer < 4:
@@ -251,9 +293,9 @@
                 part = slice(count * phase, count * (phase + 1))
                 target[part, span] = masked(values[part], phase, start).astype(BF)
 
-    for start in tiles_of(8):
-        hs[:, start : start + STEP] = jnp.dot(
-            w_head[...], xb[:, start : start + STEP], preferred_element_type=F32
+    for start, width in tiles_of(8):
+        hs[:, start : start + width] = jnp.dot(
+            w_head[...], xb[:, start : start + width], preferred_element_type=F32
         )
     rows_out = []
     for g in range(5, 21):
@@ -261,24 +303,34 @@
         values = None
         for at, (pair_, tap) in enumerate(shifts):
             off = low + shift_of(pair_, tap)
-            term = hs[32 * at : 32 * at + 32, off : off + STEP]
+            term = hs[32 * at : 32 * at + 32, off : off + 256]
             values = term if values is None else values + term
         rows_out.append(values.astype(BF))
     even = jnp.concatenate([values[:16] for values in rows_out], axis=0)
     odd = jnp.concatenate([values[16:] for values in rows_out], axis=0)
-    k_at = iota((256, 256), 0)
-    n_at = iota((256, 256), 1)
-    cell = lax.shift_right_arithmetic(n_at, 1) + HALO
-    cell = jnp.where(jnp.logical_and(seam, cell >= 18), cell + 1, cell)
+    k_at = iota((256, 384), 0)
+    n_at = iota((256, 384), 1)
+    over = n_at - 256
+    turn = jnp.where(over >= 36, over - 36, jnp.where(over >= 18, over - 18, over))
+    wanted = jnp.where(over < 0, n_at, 256 + turn)
+    cell = lax.shift_right_arithmetic(wanted, 1) + HALO
     spread = [
-        jnp.where((k_at == cell) & ((n_at & 1) == b), 1.0, 0.0).astype(BF) for b in range(2)
+        jnp.where((k_at == cell) & ((wanted & 1) == b), 1.0, 0.0).astype(BF) for b in range(2)
     ]
     result = jnp.dot(even, spread[0], preferred_element_type=F32) + jnp.dot(
         odd, spread[1], preferred_element_type=F32
     )
     first = result[:, :128].reshape(32, 8, 128)
-    second = result[:, 128:].reshape(32, 8, 128)
-    top = iota((32, 8, 128), 1) < 4
+    second = result[:, 128:256].reshape(32, 8, 128)
+    sub8 = iota((32, 8, 128), 1)
+    lane8 = iota((32, 8, 128), 2)
+    low8 = 18 * (sub8 & 3)
+    extra = jnp.where(
+        (lane8 >= low8) & (lane8 < low8 + 18), result[:, 256:].reshape(32, 8, 128), 0.0
+    )
+    extra = extra + pltpu.roll(extra, 1, 1) + pltpu.roll(extra, 2, 1)
+    first = jnp.where((sub8 & 3) == 3, pltpu.roll(extra, 1, 1), first)
+    top = sub8 < 4
     even_rows = jnp.where(top, first, pltpu.roll(second, 4, 1)).astype(BF)
     odd_rows = jnp.where(top, pltpu.roll(first, 4, 1), second).astype(BF)
     for i in range(32):
@@ -286,12 +338,12 @@
         y_ref[2 * i + 1] = odd_rows[i]
 
 
-def run_main(place, ext, above, below, weights):
+def run_main(place, ext, above, below, pack):
     vmem = pl.BlockSpec(memory_space=pltpu.VMEM)
     return pl.pallas_call(
         main_kernel,
         out_shape=jax.ShapeDtypeStruct((64, 8, 128), BF),
-        in_specs=[pl.BlockSpec(memory_space=pltpu.SMEM)] + [vmem] * 12,
+        in_specs=[pl.BlockSpec(memory_space=pltpu.SMEM)] + [vmem] * 4,
         out_specs=vmem,
         scratch_shapes=[
             pltpu.VMEM((8, LANES), F32),
@@ -305,15 +357,15 @@
             pltpu.VMEM((64, LANES), BF),
             pltpu.VMEM((128, LANES), BF),
             pltpu.VMEM((384, LANES), F32),
-            pltpu.VMEM((72, LANES), F32),
+            pltpu.VMEM((80, LANES), F32),
             pltpu.VMEM((288, LANES), F32),
         ],
-        compiler_params=pltpu.CompilerParams(vmem_limit_bytes=48 << 20),
+        compiler_params=pltpu.CompilerParams(vmem_limit_bytes=44 << 20),
         cost_estimate=pl.CostEstimate(
             flops=2_000_000_000, bytes_accessed=4_000_000, transcendentals=0
         ),
         name="network",
-    )(place, ext, above, below, *weights)
+    )(place, ext, above, below, pack)
 
 
 def rows_kernel(z_ref, o_ref):
@@ -326,9 +378,12 @@
 
     count = z_ref.shape[0]
     first, second = halves(0)
-    opening = first
+    spare = z_ref[count - 1].astype(F32)[3:4]
+    closing = jnp.concatenate(
+        [pltpu.roll(spare, 110 - 18 * plane, 1) for plane in range(3)] + [spare], axis=0
+    )
     for source in range(count):
-        following = halves(source + 1) if source + 1 < count else (opening, None)
+        following = halves(source + 1) if source + 1 < count else (closing, None)
         at = 256 * source
         early = jnp.where(head, first, second)
         later = jnp.where(head, second, following[0])
@@ -353,16 +408,16 @@
 def on_device(decoded, loop_in, loop_out, first_conv, d1, d2, d3, d4, d5, head_conv):
     cols = lax.axis_size("col")
     rows = lax.axis_size("row")
-    weights = run_prep(
+    pack = run_prep(
         loop_in.transpose(0, 2, 1), loop_out, first_conv.transpose(0, 2, 1),
         d1, d2, d3, d4, d5, head_conv,
     )
-    left = lax.ppermute(decoded, "col", [(i, (i + 1) % cols) for i in range(cols)])
+    left = lax.ppermute(decoded, "col", [(i, i + 1) for i in range(cols - 1)])
     ext = jnp.stack([left, decoded])
     above = lax.ppermute(ext, "row", [(i, i + 1) for i in range(rows - 1)])
     below = lax.ppermute(ext, "row", [(i + 1, i) for i in range(rows - 1)])
     place = jnp.stack([lax.axis_index("row"), lax.axis_index("col")]).astype(jnp.int32)
-    sent = run_main(place, ext, above, below, weights)
+    sent = run_main(place, ext, above, below, pack)
     received = lax.all_to_all(sent, "col", split_axis=0, concat_axis=0, tiled=True)
     return run_rows(received).transpose(1, 0, 2)[None]
 

time: 68.9 us -> 65.1 us (0.945); the launches traced: 68.4 us -> 63.9 us
  local copies, waits for them, and re-layouts: 5.04 us -> 1.49 us
  Pallas kernels: 17.1 us -> 16.4 us
    unnamed x18 -> x2, local copies, waits for them, and re-layouts: 5.04 us -> 1.49 us
    pallas_call x1, Pallas kernels: 15 us -> 12 us  [run_main(): pl.pallas_call(main_kernel, out_shape=jax.ShapeDtypeStruct((64, 8, 128),...]
    pallas_call x1, Pallas kernels: 1.26 us -> 3.53 us  [run_prep(): pl.pallas_call(prep_kernel, out_shape=jax.ShapeDtypeStruct((1184, 768), B...]
  transfers between devices with their start and end apart: 3 -> 3, of which waited for: 1 -> 1; matrix products, arithmetic and copies ran while one was open for 0% -> 0% of each run, Pallas kernels for 2% -> 6%
where the time goes in v2:
time: 65.1 us; the launch traced here: 63.9 us
  blocking collectives  31.8 us (49%)
  Pallas kernels  16.4 us (25%)
  starting transfers between devices  12.1 us (19%)
  local copies, waits for them, and re-layouts  1.49 us (2%)
  waiting for transfers between devices  1.14 us (2%)
  other arithmetic  0.82 us (1%)
    all_to_all x1, blocking collectives, on_device(): lax.all_to_all(sent, 'col', split_axis=0, concat_axis=0, tiled=True)  31.8 us
    pallas_call x1, Pallas kernels, run_main(): pl.pallas_call(main_kernel, out_shape=jax.ShapeDtypeStruct((64, 8, 128),...  12 us
    ppermute x1, starting transfers between devices, on_device(): above = lax.ppermute(ext, 'row', [(i, i + 1) for i in range(rows - 1)])  4.94 us
    ppermute x1, starting transfers between devices, on_device(): left = lax.ppermute(decoded, 'col', [(i, i + 1) for i in range(cols - 1)])  4.77 us
    pallas_call x1, Pallas kernels, run_prep(): pl.pallas_call(prep_kernel, out_shape=jax.ShapeDtypeStruct((1184, 768), B...  3.53 us
    ppermute x1, starting transfers between devices, on_device(): below = lax.ppermute(ext, 'row', [(i + 1, i) for i in range(rows - 1)])  2.44 us
    unnamed x2, local copies, waits for them, and re-layouts  1.49 us
  transfers between devices with their start and end apart: 3, of which 1 were waited for; matrix products, arithmetic and copies ran while one was open for 0% of the time, Pallas kernels for 6%

profile of v2, /device:TPU:7, one launch (start us, length us, event | category | flops | bytes accessed | tf_op | source)
XLA Modules:
  0.0 63.9 jit_solution(4534871894508218850)
XLA Ops:
  0.0 4.8 %collective-permute-start = (bf16[3,32,128]{2,1,0:T(8,128)(2,1)}, bf16[3,32,128]{2,1,0:T(8,128)(2,1)S(1)}, u32[]{:S(2)}, u32[]{:S(2)}) collective-permute-start(bf16[3,32,128]{2,1,0:T(8,128)(2,1)} %param.10), channel_id=1, source_target_pairs={{0,8},{8,16},{16,24},{24,32},{32,40},{40,48},{48,56},{56,64},{64,7... | collective-permute-start | bytes 73736 | tf_op jit(solution)/shard_map/ppermute | solution.py:415
  4.8 1.1 %collective-permute-done = bf16[3,32,128]{2,1,0:T(8,128)(2,1)S(1)} collective-permute-done((bf16[3,32,128]{2,1,0:T(8,128)(2,1)}, bf16[3,32,128]{2,1,0:T(8,128)(2,1)S(1)}, u32[]{:S(2)}, u32[]{:S(2)}) %collective-permute-start) | collective-permute-done | bytes 24608 | tf_op jit(solution)/shard_map/ppermute | solution.py:415
  5.9 0.7 %pad_maximum_fusion.ext = bf16[2,3,32,128]{3,2,1,0:T(8,128)(2,1)S(1)} fusion(bf16[1,3,32,128]{3,2,1,0:T(8,128)(2,1)} %bitcast.9, bf16[1,3,32,128]{3,2,1,0:T(8,128)(2,1)S(1)} %bitcast.10), kind=kLoop, calls=%fused_computation | loop fusion | flops 24576 | bytes 98304 | tf_op jit(solution)/shard_map/stack | solution.py:416
  6.7 2.4 %collective-permute-start.2 = (bf16[2,3,32,128]{3,2,1,0:T(8,128)(2,1)S(1)}, bf16[2,3,32,128]{3,2,1,0:T(8,128)(2,1)S(1)}, u32[]{:S(2)}, u32[]{:S(2)}) collective-permute-start(bf16[2,3,32,128]{3,2,1,0:T(8,128)(2,1)S(1)} %pad_maximum_fusion.ext), channel_id=1, source_target_pairs={{1,0},{2,1},{3,2},{4,3},{5,4},{6,5},{7,6},{9,8},{10,9},{11,10},{12... | collective-permute-start | bytes 147464 | tf_op jit(solution)/shard_map/ppermute | solution.py:418
  9.1 4.9 %collective-permute-start.1 = (bf16[2,3,32,128]{3,2,1,0:T(8,128)(2,1)S(1)}, bf16[2,3,32,128]{3,2,1,0:T(8,128)(2,1)S(1)}, u32[]{:S(2)}, u32[]{:S(2)}) collective-permute-start(bf16[2,3,32,128]{3,2,1,0:T(8,128)(2,1)S(1)} %pad_maximum_fusion.ext), channel_id=1, source_target_pairs={{0,1},{1,2},{2,3},{3,4},{4,5},{5,6},{6,7},{8,9},{9,10},{10,11},{11... | collective-permute-start | bytes 147464 | tf_op jit(solution)/shard_map/ppermute | solution.py:417
  14.0 0.1 pad_add_fusion.place
  14.1 3.5 %weights.1.pack = bf16[1184,768]{1,0:T(8,128)(2,1)} custom-call(bf16[9,3,32]{2,1,0:T(4,128)(2,1)} %bitcast.11, bf16[9,3,32]{2,1,0:T(4,128)(2,1)} %refs_1_.1, bf16[9,3,64]{2,1,0:T(4,128)(2,1)} %bitcast.12, bf16[9,32,64]{2,1,0:T(8,128)(2,1)} %refs_3_.1, bf16[9,32,96]{2,1,0:T(8,128)(2,1)} %refs_4_.1, bf16[9,32,128]{2,1,0:T(8,128)(2,1)} %refs_5_.1, ...), custom_call_target="tpu_custom_call" | custom-call | flops 20000000 | bytes 3000000 | tf_op jit(solution)/shard_map/weights/pallas_call | solution.py:165
  17.7 0.0 collective-permute-done.2.below
  17.7 0.0 collective-permute-done.1.above
  17.7 0.0 copy-start
  17.7 1.5 %copy-done = bf16[1184,768]{1,0:T(8,128)(2,1)S(1)} copy-done((bf16[1184,768]{1,0:T(8,128)(2,1)S(1)}, bf16[1184,768]{1,0:T(8,128)(2,1)}, u32[]{:S(2)}) %copy-start) | copy-done | bytes 1818648
  19.2 12.0 %network.1 = bf16[64,8,128]{2,1,0:T(8,128)(2,1)S(1)} custom-call(s32[2]{0:T(128)S(1)} %pad_add_fusion.place, bf16[2,3,32,128]{3,2,1,0:T(8,128)(2,1)S(1)} %pad_maximum_fusion.ext, bf16[2,3,32,128]{3,2,1,0:T(8,128)(2,1)S(1)} %collective-permute-done.1.above, bf16[2,3,32,128]{3,2,1,0:T(8,128)(2,1)S(1)} %collective-permute-done.2.below, ...), custom_call_target="tpu_custom_call" | custom-call | flops 2000000000 | bytes 4000000 | tf_op jit(solution)/shard_map/network/pallas_call | solution.py:343
  31.2 31.8 %all_to_all.5.z_ref = bf16[64,8,128]{2,1,0:T(8,128)(2,1)S(1)} all-to-all(bf16[64,8,128]{2,1,0:T(8,128)(2,1)S(1)} %network.1), channel_id=1, replica_groups=mesh['col'=64,'row'=8] {'col'}, dimensions={0} | all-to-all | bytes 262144 | tf_op jit(solution)/shard_map/all_to_all | solution.py:421
  63.0 0.9 %rows.1 = f32[3,1,16384]{2,1,0:T(1,128)} custom-call(bf16[64,8,128]{2,1,0:T(8,128)(2,1)S(1)} %all_to_all.5.z_ref), custom_call_target="tpu_custom_call" | custom-call | tf_op jit(solution)/shard_map/rows/pallas_call | solution.py:398
Async XLA Ops:
  0.0 5.9 %collective-permute-start = (bf16[3,32,128]{2,1,0:T(8,128)(2,1)}, bf16[3,32,128]{2,1,0:T(8,128)(2,1)S(1)}, u32[]{:S(2)}, u32[]{:S(2)}) collective-permute-start(bf16[3,32,128]{2,1,0:T(8,128)(2,1)} %param.10), channel_id=1, source_target_pairs={{0,8},{8,16},{16,24},{24,32},{32,40},{40,48},{48,56},{56,64},{64,7... | collective-permute-start | bytes 73736 | tf_op jit(solution)/shard_map/ppermute | solution.py:415
  6.7 11.0 %collective-permute-start.2 = (bf16[2,3,32,128]{3,2,1,0:T(8,128)(2,1)S(1)}, bf16[2,3,32,128]{3,2,1,0:T(8,128)(2,1)S(1)}, u32[]{:S(2)}, u32[]{:S(2)}) collective-permute-start(bf16[2,3,32,128]{3,2,1,0:T(8,128)(2,1)S(1)} %pad_maximum_fusion.ext), channel_id=1, source_target_pairs={{1,0},{2,1},{3,2},{4,3},{5,4},{6,5},{7,6},{9,8},{10,9},{11,10},{12... | collective-permute-start | bytes 147464 | tf_op jit(solution)/shard_map/ppermute | solution.py:418
  9.1 8.6 %collective-permute-start.1 = (bf16[2,3,32,128]{3,2,1,0:T(8,128)(2,1)S(1)}, bf16[2,3,32,128]{3,2,1,0:T(8,128)(2,1)S(1)}, u32[]{:S(2)}, u32[]{:S(2)}) collective-permute-start(bf16[2,3,32,128]{3,2,1,0:T(8,128)(2,1)S(1)} %pad_maximum_fusion.ext), channel_id=1, source_target_pairs={{0,1},{1,2},{2,3},{3,4},{4,5},{5,6},{6,7},{8,9},{9,10},{10,11},{11... | collective-permute-start | bytes 147464 | tf_op jit(solution)/shard_map/ppermute | solution.py:417
  17.7 1.5 %copy-start = (bf16[1184,768]{1,0:T(8,128)(2,1)S(1)}, bf16[1184,768]{1,0:T(8,128)(2,1)}, u32[]{:S(2)}) copy-start(bf16[1184,768]{1,0:T(8,128)(2,1)} %weights.1.pack) | copy-start | bytes 5455876

commit v3 on v2

--- a/solution.py
+++ b/solution.py
@@ -11,6 +11,7 @@
 STRIDE = 147
 BASE = 128
 PAIRS = 26
+END = BASE + PAIRS * STRIDE
 LANES = 4096
 STEP = 1024
 HALO = 9
@@ -190,8 +191,16 @@
     w_in, w_out, w_first, w_f, w_1, w_2, w_3, w_4, w_head = sections(pack)
     row_at = place[0]
     col_at = place[1]
-    for ref in (x0, hid, fil, xf, x1, x2, x3, x4, xb, zs):
-        ref[...] = jnp.zeros(ref.shape, ref.dtype)
+    x0[:, :BASE] = jnp.zeros((8, BASE), F32)
+    x0[:, END:] = jnp.zeros((8, LANES - END), F32)
+    for layer, written in (
+        (1, (zs,)), (2, (fil,)), (3, (xf,)), (4, (x1,)), (5, (x2,)), (6, (x3,)), (7, (x4,)), (8, (hs,))
+    ):
+        spans = tiles_of(layer)
+        low, high = spans[0][0], spans[-1][0] + spans[-1][1]
+        for ref in written:
+            for side in (slice(max(low - 256, 0), low), slice(high, min(high + 256, LANES))):
+                ref[:, side] = jnp.zeros((ref.shape[0], side.stop - side.start), ref.dtype)
 
     lane = iota((8, LANES), 1) - BASE
     pair = lax.shift_right_arithmetic(lane * 28533, 22)
@@ -413,6 +422,7 @@
         d1, d2, d3, d4, d5, head_conv,
     )
     left = lax.ppermute(decoded, "col", [(i, i + 1) for i in range(cols - 1)])
+    left, pack = lax.optimization_barrier((left, pack))
     ext = jnp.stack([left, decoded])
     above = lax.ppermute(ext, "row", [(i, i + 1) for i in range(rows - 1)])
     below = lax.ppermute(ext, "row", [(i + 1, i) for i in range(rows - 1)])

time: 65.1 us -> 64.4 us (0.989)
  the two profiles are of different devices: /device:TPU:7 before, /device:TPU:9 now
where the time goes in v3:
time: 64.4 us; the launch traced here: 64.1 us
  blocking collectives  30.1 us (47%)
  Pallas kernels  16.3 us (25%)
  starting transfers between devices  11.1 us (17%)
  waiting for transfers between devices  4.94 us (8%)
  local copies, waits for them, and re-layouts  1.5 us (2%)
    all_to_all x1, blocking collectives, on_device(): lax.all_to_all(sent, 'col', split_axis=0, concat_axis=0, tiled=True)  30.1 us
    pallas_call x1, Pallas kernels, run_main(): pl.pallas_call(main_kernel, out_shape=jax.ShapeDtypeStruct((64, 8, 128),...  11.9 us
    ppermute x1, waiting for transfers between devices, on_device(): above = lax.ppermute(ext, 'row', [(i, i + 1) for i in range(rows - 1)])  4.93 us
    ppermute x1, starting transfers between devices, on_device(): left = lax.ppermute(decoded, 'col', [(i, i + 1) for i in range(cols - 1)])  4.9 us
    ppermute x1, starting transfers between devices, on_device(): below = lax.ppermute(ext, 'row', [(i + 1, i) for i in range(rows - 1)])  4.27 us
    pallas_call x1, Pallas kernels, run_prep(): pl.pallas_call(prep_kernel, out_shape=jax.ShapeDtypeStruct((1184, 768), B...  3.55 us
    ppermute x1, starting transfers between devices, on_device(): above = lax.ppermute(ext, 'row', [(i, i + 1) for i in range(rows - 1)])  1.92 us
    unnamed x4, local copies, waits for them, and re-layouts  1.5 us
  transfers between devices with their start and end apart: 3, of which 1 were waited for; matrix products, arithmetic and copies ran while one was open for 0% of the time, Pallas kernels for 6%

profile of v3, /device:TPU:9, one launch (start us, length us, event | category | flops | bytes accessed | tf_op | source)
XLA Modules:
  0.0 64.1 jit_solution(14418992154205292174)
XLA Ops:
  0.0 0.0 copy-start.1
  0.0 4.9 %collective-permute-start = (bf16[3,32,128]{2,1,0:T(8,128)(2,1)}, bf16[3,32,128]{2,1,0:T(8,128)(2,1)S(1)}, u32[]{:S(2)}, u32[]{:S(2)}) collective-permute-start(bf16[3,32,128]{2,1,0:T(8,128)(2,1)} %param.10), channel_id=1, source_target_pairs={{0,8},{8,16},{16,24},{24,32},{32,40},{40,48},{48,56},{56,64},{64,7... | collective-permute-start | bytes 73736 | tf_op jit(solution)/shard_map/ppermute | solution.py:424
  4.9 3.5 %weights.1.pack = bf16[1184,768]{1,0:T(8,128)(2,1)} custom-call(bf16[9,3,32]{2,1,0:T(4,128)(2,1)} %bitcast.11, bf16[9,3,32]{2,1,0:T(4,128)(2,1)} %refs_1_.1, bf16[9,3,64]{2,1,0:T(4,128)(2,1)} %bitcast.12, bf16[9,32,64]{2,1,0:T(8,128)(2,1)} %refs_3_.1, bf16[9,32,96]{2,1,0:T(8,128)(2,1)} %refs_4_.1, bf16[9,32,128]{2,1,0:T(8,128)(2,1)} %refs_5_.1, ...), custom_call_target="tpu_custom_call" | custom-call | flops 20000000 | bytes 3000000 | tf_op jit(solution)/shard_map/weights/pallas_call | solution.py:166
  8.5 0.0 collective-permute-done
  8.5 0.0 copy-done.1
  8.5 4.3 %collective-permute-start.2 = (bf16[2,3,32,128]{3,2,1,0:T(8,128)(2,1)S(1)}, bf16[2,3,32,128]{3,2,1,0:T(8,128)(2,1)S(1)}, u32[]{:S(2)}, u32[]{:S(2)}) collective-permute-start(bf16[2,3,32,128]{3,2,1,0:T(8,128)(2,1)S(1)} %pad_maximum_fusion.ext), channel_id=1, source_target_pairs={{1,0},{2,1},{3,2},{4,3},{5,4},{6,5},{7,6},{9,8},{10,9},{11,10},{12... | collective-permute-start | bytes 147464 | tf_op jit(solution)/shard_map/ppermute | solution.py:428
  12.8 1.9 %collective-permute-start.1 = (bf16[2,3,32,128]{3,2,1,0:T(8,128)(2,1)S(1)}, bf16[2,3,32,128]{3,2,1,0:T(8,128)(2,1)S(1)}, u32[]{:S(2)}, u32[]{:S(2)}) collective-permute-start(bf16[2,3,32,128]{3,2,1,0:T(8,128)(2,1)S(1)} %pad_maximum_fusion.ext), channel_id=1, source_target_pairs={{0,1},{1,2},{2,3},{3,4},{4,5},{5,6},{6,7},{8,9},{9,10},{10,11},{11... | collective-permute-start | bytes 147464 | tf_op jit(solution)/shard_map/ppermute | solution.py:427
  14.7 0.1 pad_add_fusion.place
  14.8 0.0 collective-permute-done.2.below
  14.8 4.9 %collective-permute-done.1.above = bf16[2,3,32,128]{3,2,1,0:T(8,128)(2,1)S(1)} collective-permute-done((bf16[2,3,32,128]{3,2,1,0:T(8,128)(2,1)S(1)}, bf16[2,3,32,128]{3,2,1,0:T(8,128)(2,1)S(1)}, u32[]{:S(2)}, u32[]{:S(2)}) %collective-permute-start.1) | collective-permute-done | bytes 49184 | tf_op jit(solution)/shard_map/ppermute | solution.py:427
  19.7 0.0 copy-start
  19.7 1.5 %copy-done = bf16[1184,768]{1,0:T(8,128)(2,1)S(1)} copy-done((bf16[1184,768]{1,0:T(8,128)(2,1)S(1)}, bf16[1184,768]{1,0:T(8,128)(2,1)}, u32[]{:S(2)}) %copy-start) | copy-done | bytes 1818648
  21.2 11.9 %network.1 = bf16[64,8,128]{2,1,0:T(8,128)(2,1)S(1)} custom-call(s32[2]{0:T(128)S(1)} %pad_add_fusion.place, bf16[2,3,32,128]{3,2,1,0:T(8,128)(2,1)S(1)} %pad_maximum_fusion.ext, bf16[2,3,32,128]{3,2,1,0:T(8,128)(2,1)S(1)} %collective-permute-done.1.above, bf16[2,3,32,128]{3,2,1,0:T(8,128)(2,1)S(1)} %collective-permute-done.2.below, ...), custom_call_target="tpu_custom_call" | custom-call | flops 2000000000 | bytes 4000000 | tf_op jit(solution)/shard_map/network/pallas_call | solution.py:352
  33.1 30.1 %all_to_all.5.z_ref = bf16[64,8,128]{2,1,0:T(8,128)(2,1)S(1)} all-to-all(bf16[64,8,128]{2,1,0:T(8,128)(2,1)S(1)} %network.1), channel_id=1, replica_groups=mesh['col'=64,'row'=8] {'col'}, dimensions={0} | all-to-all | bytes 262144 | tf_op jit(solution)/shard_map/all_to_all | solution.py:431
  63.2 0.9 %rows.1 = f32[3,1,16384]{2,1,0:T(1,128)} custom-call(bf16[64,8,128]{2,1,0:T(8,128)(2,1)S(1)} %all_to_all.5.z_ref), custom_call_target="tpu_custom_call" | custom-call | tf_op jit(solution)/shard_map/rows/pallas_call | solution.py:407
  (1 shorter events, 0.0 us)
Async XLA Ops:
  0.0 8.5 %copy-start.1 = (bf16[3,32,128]{2,1,0:T(8,128)(2,1)S(1)}, bf16[3,32,128]{2,1,0:T(8,128)(2,1)}, u32[]{:S(2)}) copy-start(bf16[3,32,128]{2,1,0:T(8,128)(2,1)} %param.10) | copy-start | bytes 73732
  0.0 8.5 %collective-permute-start = (bf16[3,32,128]{2,1,0:T(8,128)(2,1)}, bf16[3,32,128]{2,1,0:T(8,128)(2,1)S(1)}, u32[]{:S(2)}, u32[]{:S(2)}) collective-permute-start(bf16[3,32,128]{2,1,0:T(8,128)(2,1)} %param.10), channel_id=1, source_target_pairs={{0,8},{8,16},{16,24},{24,32},{32,40},{40,48},{48,56},{56,64},{64,7... | collective-permute-start | bytes 73736 | tf_op jit(solution)/shard_map/ppermute | solution.py:424
  8.5 6.3 %collective-permute-start.2 = (bf16[2,3,32,128]{3,2,1,0:T(8,128)(2,1)S(1)}, bf16[2,3,32,128]{3,2,1,0:T(8,128)(2,1)S(1)}, u32[]{:S(2)}, u32[]{:S(2)}) collective-permute-start(bf16[2,3,32,128]{3,2,1,0:T(8,128)(2,1)S(1)} %pad_maximum_fusion.ext), channel_id=1, source_target_pairs={{1,0},{2,1},{3,2},{4,3},{5,4},{6,5},{7,6},{9,8},{10,9},{11,10},{12... | collective-permute-start | bytes 147464 | tf_op jit(solution)/shard_map/ppermute | solution.py:428
  12.8 6.9 %collective-permute-start.1 = (bf16[2,3,32,128]{3,2,1,0:T(8,128)(2,1)S(1)}, bf16[2,3,32,128]{3,2,1,0:T(8,128)(2,1)S(1)}, u32[]{:S(2)}, u32[]{:S(2)}) collective-permute-start(bf16[2,3,32,128]{3,2,1,0:T(8,128)(2,1)S(1)} %pad_maximum_fusion.ext), channel_id=1, source_target_pairs={{0,1},{1,2},{2,3},{3,4},{4,5},{5,6},{6,7},{8,9},{9,10},{10,11},{11... | collective-permute-start | bytes 147464 | tf_op jit(solution)/shard_map/ppermute | solution.py:427
  19.7 1.5 %copy-start = (bf16[1184,768]{1,0:T(8,128)(2,1)S(1)}, bf16[1184,768]{1,0:T(8,128)(2,1)}, u32[]{:S(2)}) copy-start(bf16[1184,768]{1,0:T(8,128)(2,1)} %weights.1.pack) | copy-start | bytes 5455876

commit v4 on v3

--- a/solution.py
+++ b/solution.py
@@ -185,7 +185,7 @@
 
 
 def main_kernel(
-    place, ext, above, below, pack, y_ref,
+    place, left, own, above, below, pack, y_ref,
     x0, mask, hid, fil, xf, x1, x2, x3, x4, xb, acc, zs, hs,
 ):
     w_in, w_out, w_first, w_f, w_1, w_2, w_3, w_4, w_head = sections(pack)
@@ -217,18 +217,24 @@
         inside = mask[phase, :, start : start + width]
         return (values.reshape(rows // 8, 8, width) * inside[None]).reshape(rows, width)
 
-    def wide(ref, plane):
-        return jnp.concatenate([ref[0, plane], ref[1, plane]], axis=1)
-
     stacked = jnp.concatenate(
-        [wide(ref, plane) for plane in range(3) for ref in (above, ext, below)], axis=0
+        [
+            piece
+            for plane in range(3)
+            for piece in (
+                above[plane],
+                jnp.concatenate([left[plane], own[plane]], axis=1),
+                below[plane],
+            )
+        ],
+        axis=0,
     )
     rows = 8 * PAIRS
-    m_at = iota((rows, 288), 0)
-    k_at = iota((rows, 288), 1)
+    m_at = iota((rows, 192), 0)
+    k_at = iota((rows, 192), 1)
     stored = 2 * lax.shift_right_arithmetic(m_at, 3) + (lax.shift_right_arithmetic(m_at, 2) & 1)
     plane_at = m_at & 3
-    pick = (plane_at < 3) & (stored >= 1) & (stored <= 50) & (k_at == plane_at * 96 + stored + 22)
+    pick = (plane_at < 3) & (stored >= 1) & (stored <= 50) & (k_at == plane_at * 64 + stored + 6)
     ordered = jnp.dot(
         jnp.where(pick, 1.0, 0.0).astype(BF), stacked, preferred_element_type=F32
     ).astype(BF)
@@ -347,12 +353,12 @@
         y_ref[2 * i + 1] = odd_rows[i]
 
 
-def run_main(place, ext, above, below, pack):
+def run_main(place, left, own, above, below, pack):
     vmem = pl.BlockSpec(memory_space=pltpu.VMEM)
     return pl.pallas_call(
         main_kernel,
         out_shape=jax.ShapeDtypeStruct((64, 8, 128), BF),
-        in_specs=[pl.BlockSpec(memory_space=pltpu.SMEM)] + [vmem] * 4,
+        in_specs=[pl.BlockSpec(memory_space=pltpu.SMEM)] + [vmem] * 5,
         out_specs=vmem,
         scratch_shapes=[
             pltpu.VMEM((8, LANES), F32),
@@ -374,7 +380,25 @@
             flops=2_000_000_000, bytes_accessed=4_000_000, transcendentals=0
         ),
         name="network",
-    )(place, ext, above, below, pack)
+    )(place, left, own, above, below, pack)
+
+
+def edges_kernel(left, own, top, bottom):
+    for target, rows in ((top, slice(0, 16)), (bottom, slice(16, 32))):
+        target[:, :, :128] = left[:, rows, :]
+        target[:, :, 128:] = own[:, rows, :]
+
+
+def run_edges(left, own):
+    vmem = pl.BlockSpec(memory_space=pltpu.VMEM)
+    return pl.pallas_call(
+        edges_kernel,
+        out_shape=[jax.ShapeDtypeStruct((3, 16, 256), BF)] * 2,
+        in_specs=[vmem] * 2,
+        out_specs=[vmem] * 2,
+        compiler_params=pltpu.CompilerParams(vmem_limit_bytes=8 << 20),
+        name="edges",
+    )(left, own)
 
 
 def rows_kernel(z_ref, o_ref):
@@ -423,11 +447,11 @@
     )
     left = lax.ppermute(decoded, "col", [(i, i + 1) for i in range(cols - 1)])
     left, pack = lax.optimization_barrier((left, pack))
-    ext = jnp.stack([left, decoded])
-    above = lax.ppermute(ext, "row", [(i, i + 1) for i in range(rows - 1)])
-    below = lax.ppermute(ext, "row", [(i + 1, i) for i in range(rows - 1)])
+    top, bottom = run_edges(left, decoded)
+    above = lax.ppermute(bottom, "row", [(i, i + 1) for i in range(rows - 1)])
+    below = lax.ppermute(top, "row", [(i + 1, i) for i in range(rows - 1)])
     place = jnp.stack([lax.axis_index("row"), lax.axis_index("col")]).astype(jnp.int32)
-    sent = run_main(place, ext, above, below, pack)
+    sent = run_main(place, left, decoded, above, below, pack)
     received = lax.all_to_all(sent, "col", split_axis=0, concat_axis=0, tiled=True)
     return run_rows(received).transpose(1, 0, 2)[None]
 

time: 64.4 us -> 62 us (0.963)
  the two profiles are of different devices: /device:TPU:9 before, /device:TPU:7 now
where the time goes in v4:
time: 62 us; the launch traced here: 61.8 us
  blocking collectives  29.3 us (47%)
  Pallas kernels  16.2 us (26%)
  starting transfers between devices  10.2 us (16%)
  waiting for transfers between devices  4.43 us (7%)
  local copies, waits for them, and re-layouts  1.5 us (2%)
    all_to_all x1, blocking collectives, on_device(): lax.all_to_all(sent, 'col', split_axis=0, concat_axis=0, tiled=True)  29.3 us
    pallas_call x1, Pallas kernels, run_main(): pl.pallas_call(main_kernel, out_shape=jax.ShapeDtypeStruct((64, 8, 128),...  11.8 us
    ppermute x1, starting transfers between devices, on_device(): left = lax.ppermute(decoded, 'col', [(i, i + 1) for i in range(cols - 1)])  4.9 us
    ppermute x1, waiting for transfers between devices, on_device(): below = lax.ppermute(top, 'row', [(i + 1, i) for i in range(rows - 1)])  4.43 us
    pallas_call x1, Pallas kernels, run_prep(): pl.pallas_call(prep_kernel, out_shape=jax.ShapeDtypeStruct((1184, 768), B...  3.54 us
    ppermute x1, starting transfers between devices, on_device(): above = lax.ppermute(bottom, 'row', [(i, i + 1) for i in range(rows - 1)])  3.12 us
    ppermute x1, starting transfers between devices, on_device(): below = lax.ppermute(top, 'row', [(i + 1, i) for i in range(rows - 1)])  2.16 us
    unnamed x4, local copies, waits for them, and re-layouts  1.5 us
  transfers between devices with their start and end apart: 3, of which 1 were waited for; matrix products, arithmetic and copies ran while one was open for 0% of the time, Pallas kernels for 6%

profile of v4, /device:TPU:7, one launch (start us, length us, event | category | flops | bytes accessed | tf_op | source)
XLA Modules:
  0.0 61.8 jit_solution(10273659527993876589)
XLA Ops:
  0.0 0.0 copy-start.1
  0.0 4.9 %collective-permute-start = (bf16[3,32,128]{2,1,0:T(8,128)(2,1)}, bf16[3,32,128]{2,1,0:T(8,128)(2,1)S(1)}, u32[]{:S(2)}, u32[]{:S(2)}) collective-permute-start(bf16[3,32,128]{2,1,0:T(8,128)(2,1)} %own.3), channel_id=1, source_target_pairs={{0,8},{8,16},{16,24},{24,32},{32,40},{40,48},{48,56},{56,64},{64,7... | collective-permute-start | bytes 73736 | tf_op jit(solution)/shard_map/ppermute | solution.py:448
  4.9 3.5 %weights.1.pack = bf16[1184,768]{1,0:T(8,128)(2,1)} custom-call(bf16[9,3,32]{2,1,0:T(4,128)(2,1)} %bitcast.7, bf16[9,3,32]{2,1,0:T(4,128)(2,1)} %refs_1_.1, bf16[9,3,64]{2,1,0:T(4,128)(2,1)} %bitcast.8, bf16[9,32,64]{2,1,0:T(8,128)(2,1)} %refs_3_.1, bf16[9,32,96]{2,1,0:T(8,128)(2,1)} %refs_4_.1, bf16[9,32,128]{2,1,0:T(8,128)(2,1)} %refs_5_.1, ...), custom_call_target="tpu_custom_call" | custom-call | flops 20000000 | bytes 3000000 | tf_op jit(solution)/shard_map/weights/pallas_call | solution.py:166
  8.5 0.0 collective-permute-done.left
  8.5 0.0 copy-done.1
  8.5 3.1 %collective-permute-start.1 = (bf16[3,16,256]{2,1,0:T(8,128)(2,1)S(1)}, bf16[3,16,256]{2,1,0:T(8,128)(2,1)S(1)}, u32[]{:S(2)}, u32[]{:S(2)}) collective-permute-start(bf16[3,16,256]{2,1,0:T(8,128)(2,1)S(1)} %get-tuple-element.10), channel_id=1, source_target_pairs={{0,1},{1,2},{2,3},{3,4},{4,5},{5,6},{6,7},{8,9},{9,10},{10,11},{11... | collective-permute-start | bytes 73736 | tf_op jit(solution)/shard_map/ppermute | solution.py:451
  11.6 2.2 %collective-permute-start.2 = (bf16[3,16,256]{2,1,0:T(8,128)(2,1)S(1)}, bf16[3,16,256]{2,1,0:T(8,128)(2,1)S(1)}, u32[]{:S(2)}, u32[]{:S(2)}) collective-permute-start(bf16[3,16,256]{2,1,0:T(8,128)(2,1)S(1)} %get-tuple-element.11), channel_id=1, source_target_pairs={{1,0},{2,1},{3,2},{4,3},{5,4},{6,5},{7,6},{9,8},{10,9},{11,10},{12... | collective-permute-start | bytes 73736 | tf_op jit(solution)/shard_map/ppermute | solution.py:452
  13.8 0.1 pad_add_fusion.place
  13.9 0.0 collective-permute-done.1.above
  13.9 4.4 %collective-permute-done.2.below = bf16[3,16,256]{2,1,0:T(8,128)(2,1)S(1)} collective-permute-done((bf16[3,16,256]{2,1,0:T(8,128)(2,1)S(1)}, bf16[3,16,256]{2,1,0:T(8,128)(2,1)S(1)}, u32[]{:S(2)}, u32[]{:S(2)}) %collective-permute-start.2) | collective-permute-done | bytes 24608 | tf_op jit(solution)/shard_map/ppermute | solution.py:452
  18.3 0.0 copy-start
  18.3 1.5 %copy-done = bf16[1184,768]{1,0:T(8,128)(2,1)S(1)} copy-done((bf16[1184,768]{1,0:T(8,128)(2,1)S(1)}, bf16[1184,768]{1,0:T(8,128)(2,1)}, u32[]{:S(2)}) %copy-start) | copy-done | bytes 1818648
  19.8 11.8 %network.1 = bf16[64,8,128]{2,1,0:T(8,128)(2,1)S(1)} custom-call(s32[2]{0:T(128)S(1)} %pad_add_fusion.place, bf16[3,32,128]{2,1,0:T(8,128)(2,1)S(1)} %collective-permute-done.left, bf16[3,32,128]{2,1,0:T(8,128)(2,1)S(1)} %copy-done.1, bf16[3,16,256]{2,1,0:T(8,128)(2,1)S(1)} %collective-permute-done.1.above, ...), custom_call_target="tpu_custom_call" | custom-call | flops 2000000000 | bytes 4000000 | tf_op jit(solution)/shard_map/network/pallas_call | solution.py:358
  31.6 29.3 %all_to_all.5.z_ref = bf16[64,8,128]{2,1,0:T(8,128)(2,1)S(1)} all-to-all(bf16[64,8,128]{2,1,0:T(8,128)(2,1)S(1)} %network.1), channel_id=1, replica_groups=mesh['col'=64,'row'=8] {'col'}, dimensions={0} | all-to-all | bytes 262144 | tf_op jit(solution)/shard_map/all_to_all | solution.py:455
  60.9 0.9 %rows.1 = f32[3,1,16384]{2,1,0:T(1,128)} custom-call(bf16[64,8,128]{2,1,0:T(8,128)(2,1)S(1)} %all_to_all.5.z_ref), custom_call_target="tpu_custom_call" | custom-call | tf_op jit(solution)/shard_map/rows/pallas_call | solution.py:431
  (1 shorter events, 0.0 us)
Async XLA Ops:
  0.0 8.5 %copy-start.1 = (bf16[3,32,128]{2,1,0:T(8,128)(2,1)S(1)}, bf16[3,32,128]{2,1,0:T(8,128)(2,1)}, u32[]{:S(2)}) copy-start(bf16[3,32,128]{2,1,0:T(8,128)(2,1)} %own.3) | copy-start | bytes 73732
  0.0 8.5 %collective-permute-start = (bf16[3,32,128]{2,1,0:T(8,128)(2,1)}, bf16[3,32,128]{2,1,0:T(8,128)(2,1)S(1)}, u32[]{:S(2)}, u32[]{:S(2)}) collective-permute-start(bf16[3,32,128]{2,1,0:T(8,128)(2,1)} %own.3), channel_id=1, source_target_pairs={{0,8},{8,16},{16,24},{24,32},{32,40},{40,48},{48,56},{56,64},{64,7... | collective-permute-start | bytes 73736 | tf_op jit(solution)/shard_map/ppermute | solution.py:448
  8.5 5.4 %collective-permute-start.1 = (bf16[3,16,256]{2,1,0:T(8,128)(2,1)S(1)}, bf16[3,16,256]{2,1,0:T(8,128)(2,1)S(1)}, u32[]{:S(2)}, u32[]{:S(2)}) collective-permute-start(bf16[3,16,256]{2,1,0:T(8,128)(2,1)S(1)} %get-tuple-element.10), channel_id=1, source_target_pairs={{0,1},{1,2},{2,3},{3,4},{4,5},{5,6},{6,7},{8,9},{9,10},{10,11},{11... | collective-permute-start | bytes 73736 | tf_op jit(solution)/shard_map/ppermute | solution.py:451
  11.6 6.7 %collective-permute-start.2 = (bf16[3,16,256]{2,1,0:T(8,128)(2,1)S(1)}, bf16[3,16,256]{2,1,0:T(8,128)(2,1)S(1)}, u32[]{:S(2)}, u32[]{:S(2)}) collective-permute-start(bf16[3,16,256]{2,1,0:T(8,128)(2,1)S(1)} %get-tuple-element.11), channel_id=1, source_target_pairs={{1,0},{2,1},{3,2},{4,3},{5,4},{6,5},{7,6},{9,8},{10,9},{11,10},{12... | collective-permute-start | bytes 73736 | tf_op jit(solution)/shard_map/ppermute | solution.py:452
  18.3 1.5 %copy-start = (bf16[1184,768]{1,0:T(8,128)(2,1)S(1)}, bf16[1184,768]{1,0:T(8,128)(2,1)}, u32[]{:S(2)}) copy-start(bf16[1184,768]{1,0:T(8,128)(2,1)} %weights.1.pack) | copy-start | bytes 5455876

commit v5 on v4

--- a/solution.py
+++ b/solution.py
@@ -184,13 +184,37 @@
     return jnp.maximum(values, 0.2 * values)
 
 
+def mask_kernel(place, pack, top, mask):
+    row_at = place[0]
+    col_at = place[1]
+    lane = iota((8, LANES), 1) - BASE
+    pair = lax.shift_right_arithmetic(lane * 28533, 22)
+    column = lane - pair * STRIDE
+    first_column = jnp.where(col_at == 0, 2 * HALO, 0)
+    across = jnp.logical_and(column >= first_column, column < STRIDE - 1)
+    for phase in range(2):
+        row = 2 * pair + phase - 1 - HALO + 32 * row_at
+        keep = jnp.logical_and(jnp.logical_and(row >= 0, row < 256), across)
+        mask[phase] = jnp.where(keep, 1.0, 0.0)
+
+
+def run_mask(place, pack, top):
+    vmem = pl.BlockSpec(memory_space=pltpu.VMEM)
+    return pl.pallas_call(
+        mask_kernel,
+        out_shape=jax.ShapeDtypeStruct((2, 8, LANES), F32),
+        in_specs=[pl.BlockSpec(memory_space=pltpu.SMEM), vmem, vmem],
+        out_specs=vmem,
+        compiler_params=pltpu.CompilerParams(vmem_limit_bytes=8 << 20),
+        name="mask",
+    )(place, pack, top)
+
+
 def main_kernel(
-    place, left, own, above, below, pack, y_ref,
-    x0, mask, hid, fil, xf, x1, x2, x3, x4, xb, acc, zs, hs,
+    mask, left, own, above, below, pack, y_ref,
+    x0, hid, fil, xf, x1, x2, x3, x4, xb, acc, zs, hs,
 ):
     w_in, w_out, w_first, w_f, w_1, w_2, w_3, w_4, w_head = sections(pack)
-    row_at = place[0]
-    col_at = place[1]
     x0[:, :BASE] = jnp.zeros((8, BASE), F32)
     x0[:, END:] = jnp.zeros((8, LANES - END), F32)
     for layer, written in (
@@ -201,16 +225,6 @@
         for ref in written:
             for side in (slice(max(low - 256, 0), low), slice(high, min(high + 256, LANES))):
                 ref[:, side] = jnp.zeros((ref.shape[0], side.stop - side.start), ref.dtype)
-
-    lane = iota((8, LANES), 1) - BASE
-    pair = lax.shift_right_arithmetic(lane * 28533, 22)
-    column = lane - pair * STRIDE
-    first_column = jnp.where(col_at == 0, 2 * HALO, 0)
-    across = jnp.logical_and(column >= first_column, column < STRIDE - 1)
-    for phase in range(2):
-        row = 2 * pair + phase - 1 - HALO + 32 * row_at
-        keep = jnp.logical_and(jnp.logical_and(row >= 0, row < 256), across)
-        mask[phase] = jnp.where(keep, 1.0, 0.0)
 
     def masked(values, phase, start):
         rows, width = values.shape
@@ -353,16 +367,15 @@
         y_ref[2 * i + 1] = odd_rows[i]
 
 
-def run_main(place, left, own, above, below, pack):
+def run_main(mask, left, own, above, below, pack):
     vmem = pl.BlockSpec(memory_space=pltpu.VMEM)
     return pl.pallas_call(
         main_kernel,
         out_shape=jax.ShapeDtypeStruct((64, 8, 128), BF),
-        in_specs=[pl.BlockSpec(memory_space=pltpu.SMEM)] + [vmem] * 5,
+        in_specs=[vmem] * 6,
         out_specs=vmem,
         scratch_shapes=[
             pltpu.VMEM((8, LANES), F32),
-            pltpu.VMEM((2, 8, LANES), F32),
             pltpu.VMEM((64, LANES), BF),
             pltpu.VMEM((8, LANES), F32),
             pltpu.VMEM((128, LANES), BF),
@@ -380,7 +393,7 @@
             flops=2_000_000_000, bytes_accessed=4_000_000, transcendentals=0
         ),
         name="network",
-    )(place, left, own, above, below, pack)
+    )(mask, left, own, above, below, pack)
 
 
 def edges_kernel(left, own, top, bottom):
@@ -451,7 +464,8 @@
     above = lax.ppermute(bottom, "row", [(i, i + 1) for i in range(rows - 1)])
     below = lax.ppermute(top, "row", [(i + 1, i) for i in range(rows - 1)])
     place = jnp.stack([lax.axis_index("row"), lax.axis_index("col")]).astype(jnp.int32)
-    sent = run_main(place, left, decoded, above, below, pack)
+    mask = run_mask(place, pack, top)
+    sent = run_main(mask, left, decoded, above, below, pack)
     received = lax.all_to_all(sent, "col", split_axis=0, concat_axis=0, tiled=True)
     return run_rows(received).transpose(1, 0, 2)[None]
 

time: 62 us -> 60.3 us (0.973)
  waiting for transfers between devices: 4.43 us -> 2.26 us
    ppermute x1, waiting for transfers between devices: 4.43 us -> 2.26 us  [on_device(): below = lax.ppermute(top, 'row', [(i + 1, i) for i in range(rows - 1)])]
    pallas_call x0 -> x1, Pallas kernels: none -> 0.66 us  [run_mask(): pl.pallas_call(mask_kernel, out_shape=jax.ShapeDtypeStruct((2, 8, LANES),...]
    unnamed x4 -> x6, local copies, waits for them, and re-layouts: 1.5 us -> 1.5 us
  transfers between devices with their start and end apart: 3 -> 3, of which waited for: 1 -> 1; matrix products, arithmetic and copies ran while one was open for 0% -> 0% of each run, Pallas kernels for 6% -> 7%
where the time goes in v5:
time: 60.3 us; the launch traced here: 59.8 us
  blocking collectives  29.4 us (49%)
  Pallas kernels  16.3 us (27%)
  starting transfers between devices  10.2 us (17%)
  waiting for transfers between devices  2.26 us (4%)
  local copies, waits for them, and re-layouts  1.5 us (2%)
    all_to_all x1, blocking collectives, on_device(): lax.all_to_all(sent, 'col', split_axis=0, concat_axis=0, tiled=True)  29.4 us
    pallas_call x1, Pallas kernels, run_main(): pl.pallas_call(main_kernel, out_shape=jax.ShapeDtypeStruct((64, 8, 128),...  11.2 us
    ppermute x1, starting transfers between devices, on_device(): left = lax.ppermute(decoded, 'col', [(i, i + 1) for i in range(cols - 1)])  4.9 us
    pallas_call x1, Pallas kernels, run_prep(): pl.pallas_call(prep_kernel, out_shape=jax.ShapeDtypeStruct((1184, 768), B...  3.54 us
    ppermute x1, starting transfers between devices, on_device(): above = lax.ppermute(bottom, 'row', [(i, i + 1) for i in range(rows - 1)])  3.12 us
    ppermute x1, waiting for transfers between devices, on_device(): below = lax.ppermute(top, 'row', [(i + 1, i) for i in range(rows - 1)])  2.26 us
    ppermute x1, starting transfers between devices, on_device(): below = lax.ppermute(top, 'row', [(i + 1, i) for i in range(rows - 1)])  2.16 us
    unnamed x6, local copies, waits for them, and re-layouts  1.5 us
  transfers between devices with their start and end apart: 3, of which 1 were waited for; matrix products, arithmetic and copies ran while one was open for 0% of the time, Pallas kernels for 7%

profile of v5, /device:TPU:7, one launch (start us, length us, event | category | flops | bytes accessed | tf_op | source)
XLA Modules:
  0.0 59.8 jit_solution(9796126589915625191)
XLA Ops:
  0.0 0.0 copy-start.2
  0.0 4.9 %collective-permute-start = (bf16[3,32,128]{2,1,0:T(8,128)(2,1)}, bf16[3,32,128]{2,1,0:T(8,128)(2,1)S(1)}, u32[]{:S(2)}, u32[]{:S(2)}) collective-permute-start(bf16[3,32,128]{2,1,0:T(8,128)(2,1)} %own.3), channel_id=1, source_target_pairs={{0,8},{8,16},{16,24},{24,32},{32,40},{40,48},{48,56},{56,64},{64,7... | collective-permute-start | bytes 73736 | tf_op jit(solution)/shard_map/ppermute | solution.py:461
  4.9 3.5 %weights.1.pack = bf16[1184,768]{1,0:T(8,128)(2,1)} custom-call(bf16[9,3,32]{2,1,0:T(4,128)(2,1)} %bitcast.7, bf16[9,3,32]{2,1,0:T(4,128)(2,1)} %refs_1_.1, bf16[9,3,64]{2,1,0:T(4,128)(2,1)} %bitcast.8, bf16[9,32,64]{2,1,0:T(8,128)(2,1)} %refs_3_.1, bf16[9,32,96]{2,1,0:T(8,128)(2,1)} %refs_4_.1, bf16[9,32,128]{2,1,0:T(8,128)(2,1)} %refs_5_.1, ...), custom_call_target="tpu_custom_call" | custom-call | flops 20000000 | bytes 3000000 | tf_op jit(solution)/shard_map/weights/pallas_call | solution.py:166
  8.5 0.0 collective-permute-done.left
  8.5 0.0 copy-done.2
  8.5 3.1 %collective-permute-start.1 = (bf16[3,16,256]{2,1,0:T(8,128)(2,1)S(1)}, bf16[3,16,256]{2,1,0:T(8,128)(2,1)S(1)}, u32[]{:S(2)}, u32[]{:S(2)}) collective-permute-start(bf16[3,16,256]{2,1,0:T(8,128)(2,1)S(1)} %get-tuple-element.12), channel_id=1, source_target_pairs={{0,1},{1,2},{2,3},{3,4},{4,5},{5,6},{6,7},{8,9},{9,10},{10,11},{11... | collective-permute-start | bytes 73736 | tf_op jit(solution)/shard_map/ppermute | solution.py:464
  11.6 2.2 %collective-permute-start.2 = (bf16[3,16,256]{2,1,0:T(8,128)(2,1)S(1)}, bf16[3,16,256]{2,1,0:T(8,128)(2,1)S(1)}, u32[]{:S(2)}, u32[]{:S(2)}) collective-permute-start(bf16[3,16,256]{2,1,0:T(8,128)(2,1)S(1)} %get-tuple-element.11.top), channel_id=1, source_target_pairs={{1,0},{2,1},{3,2},{4,3},{5,4},{6,5},{7,6},{9,8},{10,9},{11,10},{12... | collective-permute-start | bytes 73736 | tf_op jit(solution)/shard_map/ppermute | solution.py:465
  13.8 0.1 pad_add_fusion.place
  13.9 0.0 copy-start
  13.9 1.5 %copy-done = bf16[1184,768]{1,0:T(8,128)(2,1)S(1)} copy-done((bf16[1184,768]{1,0:T(8,128)(2,1)S(1)}, bf16[1184,768]{1,0:T(8,128)(2,1)}, u32[]{:S(2)}) %copy-start) | copy-done | bytes 1818648
  15.4 0.0 copy-start.1
  15.4 0.7 %mask.1 = f32[2,8,4096]{2,1,0:T(8,128)S(1)} custom-call(s32[2]{0:T(128)S(1)} %pad_add_fusion.place, bf16[1184,768]{1,0:T(8,128)(2,1)S(1)} %copy-done, bf16[3,16,256]{2,1,0:T(8,128)(2,1)S(1)} %get-tuple-element.11.top), custom_call_target="tpu_custom_call" | custom-call | tf_op jit(solution)/shard_map/mask/pallas_call | solution.py:203
  16.0 0.0 collective-permute-done.1.above
  16.0 2.3 %collective-permute-done.2.below = bf16[3,16,256]{2,1,0:T(8,128)(2,1)S(1)} collective-permute-done((bf16[3,16,256]{2,1,0:T(8,128)(2,1)S(1)}, bf16[3,16,256]{2,1,0:T(8,128)(2,1)S(1)}, u32[]{:S(2)}, u32[]{:S(2)}) %collective-permute-start.2) | collective-permute-done | bytes 24608 | tf_op jit(solution)/shard_map/ppermute | solution.py:465
  18.3 0.0 copy-done.1
  18.3 11.2 %network.1 = bf16[64,8,128]{2,1,0:T(8,128)(2,1)S(1)} custom-call(f32[2,8,4096]{2,1,0:T(8,128)S(1)} %mask.1, bf16[3,32,128]{2,1,0:T(8,128)(2,1)S(1)} %collective-permute-done.left, bf16[3,32,128]{2,1,0:T(8,128)(2,1)S(1)} %copy-done.2, bf16[3,16,256]{2,1,0:T(8,128)(2,1)S(1)} %collective-permute-done.1.above, ...), custom_call_target="tpu_custom_call" | custom-call | flops 2000000000 | bytes 4000000 | tf_op jit(solution)/shard_map/network/pallas_call | solution.py:372
  29.5 29.4 %all_to_all.5.z_ref = bf16[64,8,128]{2,1,0:T(8,128)(2,1)S(1)} all-to-all(bf16[64,8,128]{2,1,0:T(8,128)(2,1)S(1)} %network.1), channel_id=1, replica_groups=mesh['col'=64,'row'=8] {'col'}, dimensions={0} | all-to-all | bytes 262144 | tf_op jit(solution)/shard_map/all_to_all | solution.py:469
  59.0 0.9 %rows.1 = f32[3,1,16384]{2,1,0:T(1,128)} custom-call(bf16[64,8,128]{2,1,0:T(8,128)(2,1)S(1)} %all_to_all.5.z_ref), custom_call_target="tpu_custom_call" | custom-call | tf_op jit(solution)/shard_map/rows/pallas_call | solution.py:444
  (1 shorter events, 0.0 us)
Async XLA Ops:
  0.0 8.5 %copy-start.2 = (bf16[3,32,128]{2,1,0:T(8,128)(2,1)S(1)}, bf16[3,32,128]{2,1,0:T(8,128)(2,1)}, u32[]{:S(2)}) copy-start(bf16[3,32,128]{2,1,0:T(8,128)(2,1)} %own.3) | copy-start | bytes 73732
  0.0 8.5 %collective-permute-start = (bf16[3,32,128]{2,1,0:T(8,128)(2,1)}, bf16[3,32,128]{2,1,0:T(8,128)(2,1)S(1)}, u32[]{:S(2)}, u32[]{:S(2)}) collective-permute-start(bf16[3,32,128]{2,1,0:T(8,128)(2,1)} %own.3), channel_id=1, source_target_pairs={{0,8},{8,16},{16,24},{24,32},{32,40},{40,48},{48,56},{56,64},{64,7... | collective-permute-start | bytes 73736 | tf_op jit(solution)/shard_map/ppermute | solution.py:461
  8.5 7.5 %collective-permute-start.1 = (bf16[3,16,256]{2,1,0:T(8,128)(2,1)S(1)}, bf16[3,16,256]{2,1,0:T(8,128)(2,1)S(1)}, u32[]{:S(2)}, u32[]{:S(2)}) collective-permute-start(bf16[3,16,256]{2,1,0:T(8,128)(2,1)S(1)} %get-tuple-element.12), channel_id=1, source_target_pairs={{0,1},{1,2},{2,3},{3,4},{4,5},{5,6},{6,7},{8,9},{9,10},{10,11},{11... | collective-permute-start | bytes 73736 | tf_op jit(solution)/shard_map/ppermute | solution.py:464
  11.6 6.7 %collective-permute-start.2 = (bf16[3,16,256]{2,1,0:T(8,128)(2,1)S(1)}, bf16[3,16,256]{2,1,0:T(8,128)(2,1)S(1)}, u32[]{:S(2)}, u32[]{:S(2)}) collective-permute-start(bf16[3,16,256]{2,1,0:T(8,128)(2,1)S(1)} %get-tuple-element.11.top), channel_id=1, source_target_pairs={{1,0},{2,1},{3,2},{4,3},{5,4},{6,5},{7,6},{9,8},{10,9},{11,10},{12... | collective-permute-start | bytes 73736 | tf_op jit(solution)/shard_map/ppermute | solution.py:465
  13.9 1.5 %copy-start = (bf16[1184,768]{1,0:T(8,128)(2,1)S(1)}, bf16[1184,768]{1,0:T(8,128)(2,1)}, u32[]{:S(2)}) copy-start(bf16[1184,768]{1,0:T(8,128)(2,1)} %weights.1.pack) | copy-start | bytes 5455876
  15.4 2.9 %copy-start.1 = (bf16[1184,768]{1,0:T(8,128)(2,1)S(1)}, bf16[1184,768]{1,0:T(8,128)(2,1)}, u32[]{:S(2)}) copy-start(bf16[1184,768]{1,0:T(8,128)(2,1)} %weights.1.pack) | copy-start | bytes 5455876

commit v6 on v5

--- a/solution.py
+++ b/solution.py
@@ -13,7 +13,7 @@
 PAIRS = 26
 END = BASE + PAIRS * STRIDE
 LANES = 4096
-STEP = 1024
+STEP = 1280
 HALO = 9
 SOURCE = ((1, -1), (0, 0), (1, 0), (0, 1))
 

time: 60.3 us -> 60.3 us (level)
  no operation moved by 1% of the time
where the time goes in v6:
time: 60.3 us; the launch traced here: 59.8 us
  blocking collectives  29.4 us (49%)
  Pallas kernels  16.3 us (27%)
  starting transfers between devices  10.2 us (17%)
  waiting for transfers between devices  2.26 us (4%)
  local copies, waits for them, and re-layouts  1.5 us (2%)
    all_to_all x1, blocking collectives, on_device(): lax.all_to_all(sent, 'col', split_axis=0, concat_axis=0, tiled=True)  29.4 us
    pallas_call x1, Pallas kernels, run_main(): pl.pallas_call(main_kernel, out_shape=jax.ShapeDtypeStruct((64, 8, 128),...  11.2 us
    ppermute x1, starting transfers between devices, on_device(): left = lax.ppermute(decoded, 'col', [(i, i + 1) for i in range(cols - 1)])  4.9 us
    pallas_call x1, Pallas kernels, run_prep(): pl.pallas_call(prep_kernel, out_shape=jax.ShapeDtypeStruct((1184, 768), B...  3.54 us
    ppermute x1, starting transfers between devices, on_device(): above = lax.ppermute(bottom, 'row', [(i, i + 1) for i in range(rows - 1)])  3.12 us
    ppermute x1, waiting for transfers between devices, on_device(): below = lax.ppermute(top, 'row', [(i + 1, i) for i in range(rows - 1)])  2.26 us
    ppermute x1, starting transfers between devices, on_device(): below = lax.ppermute(top, 'row', [(i + 1, i) for i in range(rows - 1)])  2.16 us
    unnamed x6, local copies, waits for them, and re-layouts  1.5 us
  transfers between devices with their start and end apart: 3, of which 1 were waited for; matrix products, arithmetic and copies ran while one was open for 0% of the time, Pallas kernels for 7%

profile of v6, /device:TPU:7, one launch (start us, length us, event | category | flops | bytes accessed | tf_op | source)
XLA Modules:
  0.0 59.8 jit_solution(14489821904020857372)
XLA Ops:
  0.0 0.0 copy-start.2
  0.0 4.9 %collective-permute-start = (bf16[3,32,128]{2,1,0:T(8,128)(2,1)}, bf16[3,32,128]{2,1,0:T(8,128)(2,1)S(1)}, u32[]{:S(2)}, u32[]{:S(2)}) collective-permute-start(bf16[3,32,128]{2,1,0:T(8,128)(2,1)} %own.3), channel_id=1, source_target_pairs={{0,8},{8,16},{16,24},{24,32},{32,40},{40,48},{48,56},{56,64},{64,7... | collective-permute-start | bytes 73736 | tf_op jit(solution)/shard_map/ppermute | solution.py:461
  4.9 3.5 %weights.1.pack = bf16[1184,768]{1,0:T(8,128)(2,1)} custom-call(bf16[9,3,32]{2,1,0:T(4,128)(2,1)} %bitcast.7, bf16[9,3,32]{2,1,0:T(4,128)(2,1)} %refs_1_.1, bf16[9,3,64]{2,1,0:T(4,128)(2,1)} %bitcast.8, bf16[9,32,64]{2,1,0:T(8,128)(2,1)} %refs_3_.1, bf16[9,32,96]{2,1,0:T(8,128)(2,1)} %refs_4_.1, bf16[9,32,128]{2,1,0:T(8,128)(2,1)} %refs_5_.1, ...), custom_call_target="tpu_custom_call" | custom-call | flops 20000000 | bytes 3000000 | tf_op jit(solution)/shard_map/weights/pallas_call | solution.py:166
  8.5 0.0 collective-permute-done.left
  8.5 0.0 copy-done.2
  8.5 3.1 %collective-permute-start.1 = (bf16[3,16,256]{2,1,0:T(8,128)(2,1)S(1)}, bf16[3,16,256]{2,1,0:T(8,128)(2,1)S(1)}, u32[]{:S(2)}, u32[]{:S(2)}) collective-permute-start(bf16[3,16,256]{2,1,0:T(8,128)(2,1)S(1)} %get-tuple-element.12), channel_id=1, source_target_pairs={{0,1},{1,2},{2,3},{3,4},{4,5},{5,6},{6,7},{8,9},{9,10},{10,11},{11... | collective-permute-start | bytes 73736 | tf_op jit(solution)/shard_map/ppermute | solution.py:464
  11.6 2.2 %collective-permute-start.2 = (bf16[3,16,256]{2,1,0:T(8,128)(2,1)S(1)}, bf16[3,16,256]{2,1,0:T(8,128)(2,1)S(1)}, u32[]{:S(2)}, u32[]{:S(2)}) collective-permute-start(bf16[3,16,256]{2,1,0:T(8,128)(2,1)S(1)} %get-tuple-element.11.top), channel_id=1, source_target_pairs={{1,0},{2,1},{3,2},{4,3},{5,4},{6,5},{7,6},{9,8},{10,9},{11,10},{12... | collective-permute-start | bytes 73736 | tf_op jit(solution)/shard_map/ppermute | solution.py:465
  13.8 0.1 pad_add_fusion.place
  13.9 0.0 copy-start
  13.9 1.5 %copy-done = bf16[1184,768]{1,0:T(8,128)(2,1)S(1)} copy-done((bf16[1184,768]{1,0:T(8,128)(2,1)S(1)}, bf16[1184,768]{1,0:T(8,128)(2,1)}, u32[]{:S(2)}) %copy-start) | copy-done | bytes 1818648
  15.4 0.0 copy-start.1
  15.4 0.7 %mask.1 = f32[2,8,4096]{2,1,0:T(8,128)S(1)} custom-call(s32[2]{0:T(128)S(1)} %pad_add_fusion.place, bf16[1184,768]{1,0:T(8,128)(2,1)S(1)} %copy-done, bf16[3,16,256]{2,1,0:T(8,128)(2,1)S(1)} %get-tuple-element.11.top), custom_call_target="tpu_custom_call" | custom-call | tf_op jit(solution)/shard_map/mask/pallas_call | solution.py:203
  16.0 0.0 collective-permute-done.1.above
  16.0 2.3 %collective-permute-done.2.below = bf16[3,16,256]{2,1,0:T(8,128)(2,1)S(1)} collective-permute-done((bf16[3,16,256]{2,1,0:T(8,128)(2,1)S(1)}, bf16[3,16,256]{2,1,0:T(8,128)(2,1)S(1)}, u32[]{:S(2)}, u32[]{:S(2)}) %collective-permute-start.2) | collective-permute-done | bytes 24608 | tf_op jit(solution)/shard_map/ppermute | solution.py:465
  18.3 0.0 copy-done.1
  18.3 11.2 %network.1 = bf16[64,8,128]{2,1,0:T(8,128)(2,1)S(1)} custom-call(f32[2,8,4096]{2,1,0:T(8,128)S(1)} %mask.1, bf16[3,32,128]{2,1,0:T(8,128)(2,1)S(1)} %collective-permute-done.left, bf16[3,32,128]{2,1,0:T(8,128)(2,1)S(1)} %copy-done.2, bf16[3,16,256]{2,1,0:T(8,128)(2,1)S(1)} %collective-permute-done.1.above, ...), custom_call_target="tpu_custom_call" | custom-call | flops 2000000000 | bytes 4000000 | tf_op jit(solution)/shard_map/network/pallas_call | solution.py:372
  29.5 29.4 %all_to_all.5.z_ref = bf16[64,8,128]{2,1,0:T(8,128)(2,1)S(1)} all-to-all(bf16[64,8,128]{2,1,0:T(8,128)(2,1)S(1)} %network.1), channel_id=1, replica_groups=mesh['col'=64,'row'=8] {'col'}, dimensions={0} | all-to-all | bytes 262144 | tf_op jit(solution)/shard_map/all_to_all | solution.py:469
  58.9 0.9 %rows.1 = f32[3,1,16384]{2,1,0:T(1,128)} custom-call(bf16[64,8,128]{2,1,0:T(8,128)(2,1)S(1)} %all_to_all.5.z_ref), custom_call_target="tpu_custom_call" | custom-call | tf_op jit(solution)/shard_map/rows/pallas_call | solution.py:444
  (1 shorter events, 0.0 us)
Async XLA Ops:
  0.0 8.5 %copy-start.2 = (bf16[3,32,128]{2,1,0:T(8,128)(2,1)S(1)}, bf16[3,32,128]{2,1,0:T(8,128)(2,1)}, u32[]{:S(2)}) copy-start(bf16[3,32,128]{2,1,0:T(8,128)(2,1)} %own.3) | copy-start | bytes 73732
  0.0 8.5 %collective-permute-start = (bf16[3,32,128]{2,1,0:T(8,128)(2,1)}, bf16[3,32,128]{2,1,0:T(8,128)(2,1)S(1)}, u32[]{:S(2)}, u32[]{:S(2)}) collective-permute-start(bf16[3,32,128]{2,1,0:T(8,128)(2,1)} %own.3), channel_id=1, source_target_pairs={{0,8},{8,16},{16,24},{24,32},{32,40},{40,48},{48,56},{56,64},{64,7... | collective-permute-start | bytes 73736 | tf_op jit(solution)/shard_map/ppermute | solution.py:461
  8.5 7.5 %collective-permute-start.1 = (bf16[3,16,256]{2,1,0:T(8,128)(2,1)S(1)}, bf16[3,16,256]{2,1,0:T(8,128)(2,1)S(1)}, u32[]{:S(2)}, u32[]{:S(2)}) collective-permute-start(bf16[3,16,256]{2,1,0:T(8,128)(2,1)S(1)} %get-tuple-element.12), channel_id=1, source_target_pairs={{0,1},{1,2},{2,3},{3,4},{4,5},{5,6},{6,7},{8,9},{9,10},{10,11},{11... | collective-permute-start | bytes 73736 | tf_op jit(solution)/shard_map/ppermute | solution.py:464
  11.6 6.7 %collective-permute-start.2 = (bf16[3,16,256]{2,1,0:T(8,128)(2,1)S(1)}, bf16[3,16,256]{2,1,0:T(8,128)(2,1)S(1)}, u32[]{:S(2)}, u32[]{:S(2)}) collective-permute-start(bf16[3,16,256]{2,1,0:T(8,128)(2,1)S(1)} %get-tuple-element.11.top), channel_id=1, source_target_pairs={{1,0},{2,1},{3,2},{4,3},{5,4},{6,5},{7,6},{9,8},{10,9},{11,10},{12... | collective-permute-start | bytes 73736 | tf_op jit(solution)/shard_map/ppermute | solution.py:465
  13.9 1.5 %copy-start = (bf16[1184,768]{1,0:T(8,128)(2,1)S(1)}, bf16[1184,768]{1,0:T(8,128)(2,1)}, u32[]{:S(2)}) copy-start(bf16[1184,768]{1,0:T(8,128)(2,1)} %weights.1.pack) | copy-start | bytes 5455876
  15.4 2.9 %copy-start.1 = (bf16[1184,768]{1,0:T(8,128)(2,1)S(1)}, bf16[1184,768]{1,0:T(8,128)(2,1)}, u32[]{:S(2)}) copy-start(bf16[1184,768]{1,0:T(8,128)(2,1)} %weights.1.pack) | copy-start | bytes 5455876
